TPU v7x, 128 devices: a whole 4x4x4 slice. The times are simulated.
128 devices in a mesh: table: 64 (over z, y, x), ctx: 2 (over core).
Axes of the slice: x: 4, y: 4, z: 4, core: 2. Of those that a mesh axis runs over, the one named last changes fastest.
Arguments:
- item_table: float32 [131072, 256], P('table'), may hold values from -3 to 3
- serve_rows: int32 [4096, 128], P('table', 'ctx'), may hold values from 0 to 2047, as said below
- token_slots: int32 [64, 2048, 4], P('table', 'ctx'), may hold values from 0 to 4095
- lengths: int32 [64], P('table'), may hold values from 1 to 2048, as said below
- w_proj: bfloat16 [256, 2048], replicated, may hold values from -0.375 to 0.375
- w_out: bfloat16 [512, 256], replicated, may hold values from -0.25 to 0.25
- grad_out: bfloat16 [64, 2048, 256], P('table', 'ctx'), may hold values from -6 to 6
Outputs:
- layer_out: bfloat16 [64, 2048, 256], P('table', 'ctx')
- grad_table: float32 [131072, 256], P(('table', 'ctx'))
Inputs may be any that keep to these rules, and one draw needn't show every extreme that they name: `serve_rows`: the 64 rows that one owner serves to one requesting device are distinct. `lengths`: some history has all 2048 actions.
All inputs are finite; a program needn't handle non-finite values.
Results may differ from a plain program's by a relative error of at most 0.009.
Values may be sent and summed in bfloat16 or wider, within the bound.
A program may use at most 192 MiB of HBM per device.

v0:
```python
import jax
import jax.numpy as jnp
from jax import lax
from jax.sharding import PartitionSpec as P

HEAD = 128


epsilon = 1e-05
block_rows = 512


def silu_slope(inputs):
    sigmoid_value = jax.nn.sigmoid(inputs)
    return sigmoid_value * (1.0 + inputs * (1.0 - sigmoid_value))


def normalize(inputs):
    centred = inputs - jnp.mean(inputs, axis=-1, keepdims=True)
    inverse = lax.rsqrt(jnp.mean(centred * centred, axis=-1, keepdims=True) + epsilon)
    return (centred * inverse, inverse)


def normalize_wide(inputs):
    middle = jnp.mean(inputs, axis=-1, keepdims=True)
    square_mean = jnp.mean(inputs * inputs, axis=-1, keepdims=True)
    inverse = lax.rsqrt(square_mean - middle * middle + epsilon)
    return ((inputs - middle) * inverse, inverse)


def norm_back(gradients, normed, inverse):
    return (
        gradients
        - jnp.mean(gradients, axis=-1, keepdims=True)
        - normed * jnp.mean(gradients * normed, axis=-1, keepdims=True)
    ) * inverse


def blockwise(step_fn, carried, pieces):
    row_total = pieces[0].shape[0]

    def visit_block(step_index, current):
        offset = step_index * block_rows
        subset = tuple(
            (lax.dynamic_slice_in_dim(one_piece, offset, block_rows, 0) for one_piece in pieces)
        )
        return step_fn(current, subset, offset)

    return lax.fori_loop(0, row_total // block_rows, visit_block, carried)


def split_heads(matrix):
    return matrix.reshape(matrix.shape[0], -1, HEAD)


def scores(query_rows, key_rows):
    return jnp.einsum(
        "ihd,jhd->hij",
        split_heads(query_rows),
        split_heads(key_rows),
        preferred_element_type=jnp.float32,
    ) * HEAD ** (-0.5)


def on_device(item_table, serve_rows, token_slots, lengths, w_proj, w_out, grad_out):
    row_width = item_table.shape[1]
    served = item_table[serve_rows]
    fetched = lax.all_to_all(served, "table", split_axis=0, concat_axis=0, tiled=True)
    fetched_rows = fetched.reshape(-1, row_width)
    slot_ids = token_slots[0]
    embedded = fetched_rows[slot_ids[:, 0]]
    for feature in range(1, slot_ids.shape[1]):
        embedded = embedded + fetched_rows[slot_ids[:, feature]]
    row_count = embedded.shape[0]
    length = lengths[0]
    first_pos = lax.axis_index("ctx") * row_count
    positions = first_pos + jnp.arange(row_count, dtype=jnp.int32)
    valid_rows = positions < length
    score_scale = HEAD ** (-0.5)
    normal_x, input_inverse = normalize(embedded)
    normed_input = normal_x.astype(jnp.bfloat16)
    cotangent = grad_out[0]
    masked_g = jnp.where(valid_rows[:, None], cotangent, jnp.zeros_like(cotangent))

    def allowed(query_pos, key_pos):
        return ((key_pos[None, :] <= query_pos[:, None]) & (key_pos[None, :] < length)).astype(
            jnp.float32
        )

    def key_terms(query_block, grad_block, key_block, value_block, query_pos, key_pos):
        key_total = key_block.shape[0]
        block_width = key_block.shape[1]
        scaled = scores(query_block, key_block)
        allowed_mask = allowed(query_pos, key_pos)
        weights = (jax.nn.silu(scaled) * allowed_mask).astype(jnp.bfloat16)
        grad_v = jnp.einsum(
            "hij,ihd->jhd", weights, split_heads(grad_block), preferred_element_type=jnp.float32
        )
        grad_weights = jnp.einsum(
            "ihd,jhd->hij",
            split_heads(grad_block),
            split_heads(value_block),
            preferred_element_type=jnp.float32,
        )
        grad_scores = (grad_weights * silu_slope(scaled) * score_scale * allowed_mask).astype(
            jnp.bfloat16
        )
        grad_k = jnp.einsum(
            "hij,ihd->jhd",
            grad_scores,
            split_heads(query_block),
            preferred_element_type=jnp.float32,
        )
        grad_q = jnp.einsum(
            "hij,jhd->ihd", grad_scores, split_heads(key_block), preferred_element_type=jnp.float32
        )
        return (
            grad_q.reshape(query_block.shape[0], block_width),
            grad_k.reshape(key_total, block_width),
            grad_v.reshape(key_total, block_width),
        )

    pre_act = jnp.dot(normed_input, w_proj, preferred_element_type=jnp.float32)
    activated = jax.nn.silu(pre_act).astype(jnp.bfloat16)
    gating, values, queries, keyrows = jnp.split(activated, 4, axis=1)
    hidden_width = values.shape[1]

    def attend(current, subset, first_row):
        key_block, value_block = subset
        key_pos = first_row + jnp.arange(key_block.shape[0], dtype=jnp.int32)
        weights = (jax.nn.silu(scores(queries, key_block)) * allowed(positions, key_pos)).astype(
            jnp.bfloat16
        )
        summed = jnp.einsum(
            "hij,jhd->ihd", weights, split_heads(value_block), preferred_element_type=jnp.float32
        )
        return current + summed.reshape(row_count, hidden_width)

    zero_rows = jnp.zeros((row_count, hidden_width), jnp.float32)
    attended = blockwise(
        attend,
        zero_rows,
        (
            lax.all_gather(keyrows, "ctx", axis=0, tiled=True),
            lax.all_gather(values, "ctx", axis=0, tiled=True),
        ),
    )
    normed_out, out_inverse = normalize_wide(attended)
    gated_rows = (normed_out * gating.astype(jnp.float32)).astype(jnp.bfloat16)
    mixed_rows = jnp.dot(gated_rows, w_out, preferred_element_type=jnp.float32)
    layer_out = jnp.where(valid_rows[:, None], embedded + mixed_rows, 0.0).astype(jnp.bfloat16)
    grad_gated = jnp.einsum("td,hd->th", masked_g, w_out, preferred_element_type=jnp.float32)
    grad_gating = grad_gated * normed_out
    grad_attended = norm_back(
        grad_gated * gating.astype(jnp.float32), normed_out, out_inverse
    ).astype(jnp.bfloat16)

    def query_side(current, subset, first_row):
        key_block, value_block = subset
        key_pos = first_row + jnp.arange(key_block.shape[0], dtype=jnp.int32)
        scaled = scores(queries, key_block)
        grad_weights = jnp.einsum(
            "ihd,jhd->hij",
            split_heads(grad_attended),
            split_heads(value_block),
            preferred_element_type=jnp.float32,
        )
        grad_scores = (
            grad_weights * silu_slope(scaled) * score_scale * allowed(positions, key_pos)
        ).astype(jnp.bfloat16)
        summed = jnp.einsum(
            "hij,jhd->ihd", grad_scores, split_heads(key_block), preferred_element_type=jnp.float32
        )
        return current + summed.reshape(row_count, hidden_width)

    def both_sides(current, subset, first_row):
        query_block, key_block, value_block, grad_block = subset
        remote_total = query_block.shape[0]
        remote_pos = first_row + jnp.arange(remote_total, dtype=jnp.int32)
        grad_q_now = query_side(current[0], (key_block, value_block), first_row)
        unused_q, more_k, more_v = key_terms(
            query_block, grad_block, keyrows, values, remote_pos, positions
        )
        grad_k_now = current[1] + more_k
        grad_v_now = current[2] + more_v
        return (grad_q_now, grad_k_now, grad_v_now)

    grad_q, grad_k, grad_v = blockwise(
        both_sides,
        (zero_rows, zero_rows, zero_rows),
        (
            lax.all_gather(queries, "ctx", axis=0, tiled=True),
            lax.all_gather(keyrows, "ctx", axis=0, tiled=True),
            lax.all_gather(values, "ctx", axis=0, tiled=True),
            lax.all_gather(grad_attended, "ctx", axis=0, tiled=True),
        ),
    )
    grad_act = jnp.concatenate([grad_gating, grad_v, grad_q, grad_k], axis=1)
    grad_pre = (grad_act * silu_slope(pre_act)).astype(jnp.bfloat16)
    grad_x = jnp.einsum("tp,dp->td", grad_pre, w_proj, preferred_element_type=jnp.float32)
    grad_emb = masked_g.astype(jnp.float32) + norm_back(grad_x, normal_x, input_inverse)
    spread = jnp.broadcast_to(
        grad_emb[:, None, :], (row_count, slot_ids.shape[1], row_width)
    ).reshape(-1, row_width)
    slot_grads = jax.ops.segment_sum(
        spread, slot_ids.reshape(-1), num_segments=fetched_rows.shape[0]
    )
    returned = lax.all_to_all(
        slot_grads.reshape(fetched.shape).astype(jnp.bfloat16),
        "table",
        split_axis=0,
        concat_axis=0,
        tiled=True,
    ).astype(jnp.float32)
    owner_grads = jax.ops.segment_sum(
        returned.reshape(-1, row_width), serve_rows.reshape(-1), num_segments=item_table.shape[0]
    )
    grad_table = lax.psum_scatter(
        owner_grads.astype(jnp.bfloat16), "ctx", scatter_dimension=0, tiled=True
    ).astype(jnp.float32)
    return (layer_out[None], grad_table)


def solution(mesh):
    placed = (
        P("table", None),
        P("table", "ctx"),
        P("table", "ctx", None),
        P("table"),
        P(),
        P(),
        P("table", "ctx", None),
    )
    return jax.shard_map(
        on_device,
        mesh=mesh,
        in_specs=placed,
        out_specs=(P("table", "ctx", None), P(("table", "ctx"), None)),
        check_vma=False,
    )
```

profile of v0, /device:TPU:1, one launch (start us, length us, event | category | flops | bytes accessed | tf_op | source)
XLA Modules:
  0.0 598.0 jit_solution(5244479458885246611)
XLA Ops:
  8.8 16.2 %gather_fusion = f32[4096,256]{1,0:T(8,128)} fusion(f32[2048,256]{1,0:T(8,128)S(1)} %copy-done, s32[4096]{0:T(1024)S(1)} %broadcast_clamp_fusion), kind=kCustom, calls=%fused_computation | custom fusion | bytes 8404992 | tf_op jit(solution)/shard_map/gather | solution.py:67
  25.0 12.4 %all-to-all-start = ((f32[64,64,256]{2,1,0:T(8,128)}), f32[64,64,256]{2,1,0:T(8,128)}, u32[]{:S(2)}, u32[]{:S(2)}) async-start(f32[64,64,256]{2,1,0:T(8,128)} %bitcast.197), calls=%async_computation | async-start | bytes 8388608 | tf_op jit(solution)/shard_map/all_to_all | solution.py:68
  37.5 53.5 %all-to-all-done = f32[64,64,256]{2,1,0:T(8,128)} async-done(((f32[64,64,256]{2,1,0:T(8,128)}), f32[64,64,256]{2,1,0:T(8,128)}, u32[]{:S(2)}, u32[]{:S(2)}) %all-to-all-start) | async-done | bytes 4194336 | tf_op jit(solution)/shard_map/all_to_all | solution.py:68
  96.7 5.6 gather_fusion.3
  102.3 6.9 %gather_fusion.1 = f32[1024,256]{1,0:T(8,128)} fusion(f32[4096,256]{1,0:T(8,128)} %bitcast.2, s32[1024]{0:T(1024)S(1)} %broadcast_clamp_fusion.4), kind=kCustom, calls=%fused_computation.1 | custom fusion | bytes 2101248 | tf_op jit(solution)/shard_map/gather | solution.py:71
  109.2 6.9 %gather_fusion.2 = f32[1024,256]{1,0:T(8,128)} fusion(f32[4096,256]{1,0:T(8,128)} %bitcast.2, s32[1024]{0:T(1024)S(1)} %broadcast_clamp_fusion.3), kind=kCustom, calls=%fused_computation.2 | custom fusion | bytes 2101248 | tf_op jit(solution)/shard_map/gather | solution.py:73
  128.2 11.6 %all-gather.7.cloned.1.call-done = bf16[2048,512]{1,0:T(8,128)(2,1)} async-done(((bf16[1024,512]{1,0:T(8,128)(2,1)}), bf16[2048,512]{1,0:T(8,128)(2,1)}) %all-gather.7.cloned.1.call-update) | async-done | bytes 2097168 | tf_op jit(solution)/shard_map/all_gather | solution.py:144
  143.7 12.3 %all-gather.5.cloned.1.call-done = bf16[2048,512]{1,0:T(8,128)(2,1)} async-done(((bf16[1024,512]{1,0:T(8,128)(2,1)}), bf16[2048,512]{1,0:T(8,128)(2,1)}) %all-gather.5.cloned.1.call-update) | async-done | bytes 2097168 | tf_op jit(solution)/shard_map/all_gather | solution.py:145
  156.1 56.9 %while.32 = (s32[]{:T(128)}, f32[1024,512]{0,1:T(8,128)S(1)}, bf16[2048,512]{1,0:T(8,128)(2,1)}, bf16[2048,512]{0,1:T(8,128)(2,1)}, bf16[1024,512]{1,0:T(8,128)(...) while((s32[]{:T(128)}, f32[1024,512]{0,1:T(8,128)S(1)}, ...), condition=%wide.region_3.4_spmd.clone, body=%wide.region_2.3_spmd.clone.sunk | while | flops 1091045888 | bytes 17839300 | solution.py:49
  160.9 7.0 %fusion.133 = f32[4,128,1024]{2,1,0:T(8,128)} fusion(bf16[512,4,128]{0,2,1:T(8,128)(2,1)S(1)} %bitcast.200, f32[1024,512]{0,1:T(8,128)} %and_convert_fusion.2, bf16[512,4,128]{0,2,1:T(8,128)(2,1)S(1)} %bitcast.202, bf16[1024,512]{1,0:T(8,128)(2,1)} %get-tuple-element.704), kind=kOutput, calls=%fused_computation.16.clone.1 | convolution fusion | flops 1088421888 | bytes 6291456 | tf_op jit(solution)/shard_map/while/body/eval_jaxpr/hij,jhd->ihd/dot_general | solution.py:134
  175.3 7.0 %fusion.133 = f32[4,128,1024]{2,1,0:T(8,128)} fusion(bf16[512,4,128]{0,2,1:T(8,128)(2,1)S(1)} %bitcast.200, f32[1024,512]{0,1:T(8,128)} %and_convert_fusion.2, bf16[512,4,128]{0,2,1:T(8,128)(2,1)S(1)} %bitcast.202, bf16[1024,512]{1,0:T(8,128)(2,1)} %get-tuple-element.704), kind=kOutput, calls=%fused_computation.16.clone.1 | convolution fusion | flops 1088421888 | bytes 6291456 | tf_op jit(solution)/shard_map/while/body/eval_jaxpr/hij,jhd->ihd/dot_general | solution.py:134
  189.5 7.0 %fusion.133 = f32[4,128,1024]{2,1,0:T(8,128)} fusion(bf16[512,4,128]{0,2,1:T(8,128)(2,1)S(1)} %bitcast.200, f32[1024,512]{0,1:T(8,128)} %and_convert_fusion.2, bf16[512,4,128]{0,2,1:T(8,128)(2,1)S(1)} %bitcast.202, bf16[1024,512]{1,0:T(8,128)(2,1)} %get-tuple-element.704), kind=kOutput, calls=%fused_computation.16.clone.1 | convolution fusion | flops 1088421888 | bytes 6291456 | tf_op jit(solution)/shard_map/while/body/eval_jaxpr/hij,jhd->ihd/dot_general | solution.py:134
  203.6 7.0 %fusion.133 = f32[4,128,1024]{2,1,0:T(8,128)} fusion(bf16[512,4,128]{0,2,1:T(8,128)(2,1)S(1)} %bitcast.200, f32[1024,512]{0,1:T(8,128)} %and_convert_fusion.2, bf16[512,4,128]{0,2,1:T(8,128)(2,1)S(1)} %bitcast.202, bf16[1024,512]{1,0:T(8,128)(2,1)} %get-tuple-element.704), kind=kOutput, calls=%fused_computation.16.clone.1 | convolution fusion | flops 1088421888 | bytes 6291456 | tf_op jit(solution)/shard_map/while/body/eval_jaxpr/hij,jhd->ihd/dot_general | solution.py:134
  223.6 13.6 %all-gather.11.cloned.1.call-done = bf16[2048,512]{1,0:T(8,128)(2,1)} async-done(((bf16[1024,512]{1,0:T(8,128)(2,1)}), bf16[2048,512]{1,0:T(8,128)(2,1)}) %all-gather.11.cloned.1.call-update) | async-done | bytes 2097168 | tf_op jit(solution)/shard_map/all_gather | solution.py:195
  237.2 219.6 %while.33 = (s32[]{:T(128)}, f32[1024,512]{0,1:T(8,128)}, f32[1024,512]{0,1:T(8,128)}, f32[1024,512]{0,1:T(8,128)}, bf16[2048,512]{0,1:T(8,128)(2,1)}, /*index=5...) while((s32[]{:T(128)}, f32[1024,512]{0,1:T(8,128)}, ...), condition=%wide.region_9.10_spmd.clone, body=%wide.region_8.9_spmd.clone.sunk | while | flops 3826782720 | bytes 169898464 | solution.py:49
  247.9 10.1 %fusion.149 = f32[4,128,1024]{2,1,0:T(8,128)} fusion(bf16[512,4,128]{0,2,1:T(8,128)(2,1)S(1)} %bitcast.201, f32[4,512,1024]{2,1,0:T(8,128)} %fusion.148, f32[1024,512]{0,1:T(8,128)} %and_select_fusion.2, bf16[1024,512]{1,0:T(8,128)(2,1)} %get-tuple-element.754), kind=kOutput, calls=%fused_computation.44.clone.1 | convolution fusion | flops 1096810496 | bytes 14155776 | tf_op jit(solution)/shard_map/while/body/eval_jaxpr/hij,jhd->ihd/dot_general | solution.py:171
  275.2 10.1 %fusion.154 = f32[4,128,1024]{2,1,0:T(8,128)} fusion(bf16[512,4,128]{0,2,1:T(8,128)(2,1)S(1)} %bitcast.195, f32[4,512,1024]{2,1,0:T(8,128)} %copy-done.2, f32[512,1024]{1,0:T(8,128)} %fusion.153, bf16[512,4,128]{0,2,1:T(8,128)(2,1)S(1)} %bitcast.199, bf16[1024,4,128]{0,2,1:T(8,128)(2,1)} %bitcast.196), kind=kOutput, calls=%fused_computation.43.clone.1 | convolution fusion | flops 1096810496 | bytes 14680064 | tf_op jit(solution)/shard_map/while/body/eval_jaxpr/hij,ihd->jhd/dot_general | solution.py:108
  302.2 10.0 %fusion.149 = f32[4,128,1024]{2,1,0:T(8,128)} fusion(bf16[512,4,128]{0,2,1:T(8,128)(2,1)S(1)} %bitcast.201, f32[4,512,1024]{2,1,0:T(8,128)} %fusion.148, f32[1024,512]{0,1:T(8,128)} %and_select_fusion.2, bf16[1024,512]{1,0:T(8,128)(2,1)} %get-tuple-element.754), kind=kOutput, calls=%fused_computation.44.clone.1 | convolution fusion | flops 1096810496 | bytes 14155776 | tf_op jit(solution)/shard_map/while/body/eval_jaxpr/hij,jhd->ihd/dot_general | solution.py:171
  329.5 10.1 %fusion.154 = f32[4,128,1024]{2,1,0:T(8,128)} fusion(bf16[512,4,128]{0,2,1:T(8,128)(2,1)S(1)} %bitcast.195, f32[4,512,1024]{2,1,0:T(8,128)} %copy-done.2, f32[512,1024]{1,0:T(8,128)} %fusion.153, bf16[512,4,128]{0,2,1:T(8,128)(2,1)S(1)} %bitcast.199, bf16[1024,4,128]{0,2,1:T(8,128)(2,1)} %bitcast.196), kind=kOutput, calls=%fused_computation.43.clone.1 | convolution fusion | flops 1096810496 | bytes 14680064 | tf_op jit(solution)/shard_map/while/body/eval_jaxpr/hij,ihd->jhd/dot_general | solution.py:108
  339.6 5.8 bitcast_add_fusion.9
  357.2 10.1 %fusion.149 = f32[4,128,1024]{2,1,0:T(8,128)} fusion(bf16[512,4,128]{0,2,1:T(8,128)(2,1)S(1)} %bitcast.201, f32[4,512,1024]{2,1,0:T(8,128)} %fusion.148, f32[1024,512]{0,1:T(8,128)} %and_select_fusion.2, bf16[1024,512]{1,0:T(8,128)(2,1)} %get-tuple-element.754), kind=kOutput, calls=%fused_computation.44.clone.1 | convolution fusion | flops 1096810496 | bytes 14155776 | tf_op jit(solution)/shard_map/while/body/eval_jaxpr/hij,jhd->ihd/dot_general | solution.py:171
  384.4 10.1 %fusion.154 = f32[4,128,1024]{2,1,0:T(8,128)} fusion(bf16[512,4,128]{0,2,1:T(8,128)(2,1)S(1)} %bitcast.195, f32[4,512,1024]{2,1,0:T(8,128)} %copy-done.2, f32[512,1024]{1,0:T(8,128)} %fusion.153, bf16[512,4,128]{0,2,1:T(8,128)(2,1)S(1)} %bitcast.199, bf16[1024,4,128]{0,2,1:T(8,128)(2,1)} %bitcast.196), kind=kOutput, calls=%fused_computation.43.clone.1 | convolution fusion | flops 1096810496 | bytes 14680064 | tf_op jit(solution)/shard_map/while/body/eval_jaxpr/hij,ihd->jhd/dot_general | solution.py:108
  394.5 5.8 bitcast_add_fusion.9
  412.2 10.1 %fusion.149 = f32[4,128,1024]{2,1,0:T(8,128)} fusion(bf16[512,4,128]{0,2,1:T(8,128)(2,1)S(1)} %bitcast.201, f32[4,512,1024]{2,1,0:T(8,128)} %fusion.148, f32[1024,512]{0,1:T(8,128)} %and_select_fusion.2, bf16[1024,512]{1,0:T(8,128)(2,1)} %get-tuple-element.754), kind=kOutput, calls=%fused_computation.44.clone.1 | convolution fusion | flops 1096810496 | bytes 14155776 | tf_op jit(solution)/shard_map/while/body/eval_jaxpr/hij,jhd->ihd/dot_general | solution.py:171
  439.4 10.1 %fusion.154 = f32[4,128,1024]{2,1,0:T(8,128)} fusion(bf16[512,4,128]{0,2,1:T(8,128)(2,1)S(1)} %bitcast.195, f32[4,512,1024]{2,1,0:T(8,128)} %copy-done.2, f32[512,1024]{1,0:T(8,128)} %fusion.153, bf16[512,4,128]{0,2,1:T(8,128)(2,1)S(1)} %bitcast.199, bf16[1024,4,128]{0,2,1:T(8,128)(2,1)} %bitcast.196), kind=kOutput, calls=%fused_computation.43.clone.1 | convolution fusion | flops 1096810496 | bytes 14680064 | tf_op jit(solution)/shard_map/while/body/eval_jaxpr/hij,ihd->jhd/dot_general | solution.py:108
  449.5 5.8 bitcast_add_fusion.9
  464.8 8.0 %fusion.83 = (f32[1024]{0:T(1024)S(1)}, f32[1024,256]{0,1:T(8,128)}) fusion(bf16[256,2048]{1,0:T(8,128)(2,1)S(1)} %copy-done.32, f32[1024,512]{1,0:T(8,128)S(1)} %copy-done.14, f32[1024,512]{1,0:T(8,128)} %copy.44, f32[1024,512]{1,0:T(8,128)} %copy.43, f32[1024,512]{1,0:T(8,128)} %get-tuple-element.528, f32[1024,2048]{1,0:T(8,128)} %get-tuple-element.540), kind=kOutput, calls=%fused_computation.138 | convolution fusion | flops 1099168768 | bytes 18878464 | tf_op jit(solution)/shard_map/tp,dp->td/dot_general | solution.py:200
  484.5 25.1 %scatter_custom_fusion = f32[4096,256]{1,0:T(8,128)} fusion(s32[4096]{0:T(1024)} %reshape.392, f32[4096,256]{1,0:T(8,128)} %reshape.394, f32[]{:T(128)} %constant.121.clone.1), kind=kCustom, calls=%fused_computation.88 | custom fusion | flops 1048576 | bytes 4194816 | tf_op jit(solution)/shard_map/scatter-add | solution.py:205
  513.4 10.3 %all-to-all-start.1 = ((bf16[64,64,256]{2,1,0:T(8,128)(2,1)}), bf16[64,64,256]{2,1,0:T(8,128)(2,1)S(1)}, u32[]{:S(2)}, u32[]{:S(2)}) async-start(bf16[64,64,256]{2,1,0:T(8,128)(2,1)} %bitcast.10), calls=%async_computation.1 | async-start | bytes 4194304 | tf_op jit(solution)/shard_map/all_to_all | solution.py:208
  523.8 29.2 %all-to-all-done.1 = bf16[64,64,256]{2,1,0:T(8,128)(2,1)S(1)} async-done(((bf16[64,64,256]{2,1,0:T(8,128)(2,1)}), bf16[64,64,256]{2,1,0:T(8,128)(2,1)S(1)}, u32[]{:S(2)}, u32[]{:S(2)}) %all-to-all-start.1) | async-done | bytes 2097184 | tf_op jit(solution)/shard_map/all_to_all | solution.py:208
  553.0 24.1 %scatter_custom_fusion.1 = f32[2048,256]{1,0:T(8,128)} fusion(s32[4096]{0:T(1024)S(1)} %reshape.400, bf16[4096,256]{1,0:T(8,128)(2,1)S(1)} %bitcast.203, f32[]{:T(128)} %constant.121.clone.1), kind=kCustom, calls=%fused_computation.80 | custom fusion | flops 2097152 | bytes 4194308 | tf_op jit(solution)/shard_map/scatter-add | solution.py:215
  583.2 6.0 %reduce-scatter.2.cloned.1.call-done = bf16[1024,256]{1,0:T(8,128)(2,1)} async-done(((bf16[2048,256]{1,0:T(8,128)(2,1)}), bf16[1024,256]{1,0:T(8,128)(2,1)}) %reduce-scatter.2.cloned.1.call-update) | async-done | bytes 524304 | tf_op jit(solution)/shard_map/reduce_scatter | solution.py:218
  (268 shorter events, 214.2 us)
Async XLA Ops:
  25.0 12.4 %copy-start.20 = (s32[1,1024,4]{1,2,0:T(4,128)S(1)}, s32[1,1024,4]{1,2,0:T(4,128)}, u32[]{:S(2)}) copy-start(s32[1,1024,4]{1,2,0:T(4,128)} %param.13) | copy-start | bytes 49156
  25.0 66.0 %all-to-all-start = ((f32[64,64,256]{2,1,0:T(8,128)}), f32[64,64,256]{2,1,0:T(8,128)}, u32[]{:S(2)}, u32[]{:S(2)}) async-start(f32[64,64,256]{2,1,0:T(8,128)} %bitcast.197), calls=%async_computation | async-start | bytes 8388608 | tf_op jit(solution)/shard_map/all_to_all | solution.py:68
  37.4 102.4 %all-gather.7.cloned.1.call-start = ((), (), s32[]{:S(2)}) async-start(), calls=%async_computation.4 | async-start | bytes 3145728 | tf_op jit(solution)/shard_map/all_gather | solution.py:144
  118.0 5.3 copy-start.10
  118.0 5.2 copy-start.21
  118.4 4.8 copy-start.27
  126.2 29.9 %all-gather.5.cloned.1.call-start = ((), (), s32[]{:S(2)}) async-start(), calls=%async_computation.3 | async-start | bytes 3145728 | tf_op jit(solution)/shard_map/all_gather | solution.py:145
  126.9 96.6 %all-gather.9.cloned.1.call-start = ((), (), s32[]{:S(2)}) async-start(), calls=%async_computation.5 | async-start | bytes 3145728 | tf_op jit(solution)/shard_map/all_gather | solution.py:192
  127.6 87.6 %copy-start.29 = (pred[1024]{0:T(1024)(128)(4,1)}, pred[1024]{0:T(1024)(128)(4,1)S(1)}, u32[]{:S(2)}) copy-start(pred[1024]{0:T(1024)(128)(4,1)S(1)} %add_compare_fusion) | copy-start | bytes 3076
  127.7 109.5 %all-gather.11.cloned.1.call-start = ((), (), s32[]{:S(2)}) async-start(), calls=%async_computation.6 | async-start | bytes 3145728 | tf_op jit(solution)/shard_map/all_gather | solution.py:195
  156.1 59.2 %copy-start.17 = (bf16[512,256]{1,0:T(8,128)(2,1)S(1)}, bf16[512,256]{1,0:T(8,128)(2,1)}, u32[]{:S(2)}) copy-start(bf16[512,256]{1,0:T(8,128)(2,1)} %param.16) | copy-start | bytes 786436
  215.2 4.0 copy-start.23
  215.2 4.0 copy-start.25
  247.9 10.1 %copy-start.3 = (f32[1024,512]{0,1:T(8,128)S(1)}, f32[1024,512]{0,1:T(8,128)}, u32[]{:S(2)}) copy-start(f32[1024,512]{0,1:T(8,128)} %get-tuple-element.730) | copy-start | bytes 6291460 | tf_op jit(solution)/shard_map/while
  260.3 3.8 copy-start.4
  266.6 5.5 copy-start.2
  275.1 10.1 %copy-start.6 = (f32[1024,512]{0,1:T(8,128)S(1)}, f32[1024,512]{0,1:T(8,128)}, u32[]{:S(2)}) copy-start(f32[1024,512]{0,1:T(8,128)} %get-tuple-element.731) | copy-start | bytes 6291460 | tf_op jit(solution)/shard_map/while
  302.2 10.0 %copy-start.3 = (f32[1024,512]{0,1:T(8,128)S(1)}, f32[1024,512]{0,1:T(8,128)}, u32[]{:S(2)}) copy-start(f32[1024,512]{0,1:T(8,128)} %get-tuple-element.730) | copy-start | bytes 6291460 | tf_op jit(solution)/shard_map/while
  321.0 5.5 copy-start.2
  329.5 10.1 %copy-start.6 = (f32[1024,512]{0,1:T(8,128)S(1)}, f32[1024,512]{0,1:T(8,128)}, u32[]{:S(2)}) copy-start(f32[1024,512]{0,1:T(8,128)} %get-tuple-element.731) | copy-start | bytes 6291460 | tf_op jit(solution)/shard_map/while
  357.2 10.1 %copy-start.3 = (f32[1024,512]{0,1:T(8,128)S(1)}, f32[1024,512]{0,1:T(8,128)}, u32[]{:S(2)}) copy-start(f32[1024,512]{0,1:T(8,128)} %get-tuple-element.730) | copy-start | bytes 6291460 | tf_op jit(solution)/shard_map/while
  369.6 3.8 copy-start.4
  375.9 5.5 copy-start.2
  384.4 10.1 %copy-start.6 = (f32[1024,512]{0,1:T(8,128)S(1)}, f32[1024,512]{0,1:T(8,128)}, u32[]{:S(2)}) copy-start(f32[1024,512]{0,1:T(8,128)} %get-tuple-element.731) | copy-start | bytes 6291460 | tf_op jit(solution)/shard_map/while
  412.2 10.1 %copy-start.3 = (f32[1024,512]{0,1:T(8,128)S(1)}, f32[1024,512]{0,1:T(8,128)}, u32[]{:S(2)}) copy-start(f32[1024,512]{0,1:T(8,128)} %get-tuple-element.730) | copy-start | bytes 6291460 | tf_op jit(solution)/shard_map/while
  424.6 3.8 copy-start.4
  430.9 5.5 copy-start.2
  439.4 10.1 %copy-start.6 = (f32[1024,512]{0,1:T(8,128)S(1)}, f32[1024,512]{0,1:T(8,128)}, u32[]{:S(2)}) copy-start(f32[1024,512]{0,1:T(8,128)} %get-tuple-element.731) | copy-start | bytes 6291460 | tf_op jit(solution)/shard_map/while
  513.4 10.3 %copy-start.19 = (s32[64,64]{1,0:T(8,128)S(1)}, s32[64,64]{1,0:T(8,128)}, u32[]{:S(2)}) copy-start(s32[64,64]{1,0:T(8,128)} %param.12) | copy-start | bytes 49156
  513.4 39.6 %all-to-all-start.1 = ((bf16[64,64,256]{2,1,0:T(8,128)(2,1)}), bf16[64,64,256]{2,1,0:T(8,128)(2,1)S(1)}, u32[]{:S(2)}, u32[]{:S(2)}) async-start(bf16[64,64,256]{2,1,0:T(8,128)(2,1)} %bitcast.10), calls=%async_computation.1 | async-start | bytes 4194304 | tf_op jit(solution)/shard_map/all_to_all | solution.py:208
  523.6 65.6 %reduce-scatter.2.cloned.1.call-start = ((), (), s32[]{:S(2)}) async-start(), calls=%async_computation.7 | async-start | bytes 1572864 | tf_op jit(solution)/shard_map/reduce_scatter | solution.py:218
  579.8 11.5 %copy-start.1 = (f32[2048,256]{1,0:T(8,128)S(1)}, f32[2048,256]{1,0:T(8,128)}, u32[]{:S(2)}) copy-start(f32[2048,256]{1,0:T(8,128)} %param.11) | copy-start | bytes 6291460
  (29 other events, 58.3 us)
Sparse Core Ops, SparseCore 0:
  126.3 13.4 all-gather.6
  141.4 14.6 all-gather.4
  157.7 14.6 all-gather.8
  222.5 14.6 all-gather.10
  579.9 9.2 reduce-scatter.1
where the time goes:
time: 605 us; the launch traced here: 598 us
  matrix products  176 us (29%)
  other arithmetic  138 us (23%)
  waiting for transfers between devices  127 us (21%)
  local copies, waits for them, and re-layouts  118 us (20%)
  starting transfers between devices  23.3 us (4%)
  between operations  15.1 us (2%)
    all_to_all x1, waiting for transfers between devices, on_device(): lax.all_to_all(served, 'table', split_axis=0, concat_axis=0, tiled=True)  53.5 us
    dot_general x4, matrix products, key_terms(): jnp.einsum('hij,ihd->jhd', grad_scores, split_heads(query_block), preferr...  40.4 us
    dot_general x4, matrix products, query_side(): jnp.einsum('hij,jhd->ihd', grad_scores, split_heads(key_block), preferred...  40.2 us
    all_to_all x1, waiting for transfers between devices, on_device(): lax.all_to_all(slot_grads.reshape(fetched.shape).astype(jnp.bfloat16), 't...  29.2 us
    dynamic_slice x32, local copies, waits for them, and re-layouts, visit_block(): lax.dynamic_slice_in_dim(one_piece, offset, block_rows, 0)  28.9 us
    dot_general x4, matrix products, attend(): jnp.einsum('hij,jhd->ihd', weights, split_heads(value_block), preferred_e...  28.2 us
    scatter-add x1, other arithmetic, on_device(): jax.ops.segment_sum(spread, slot_ids.reshape(-1), num_segments=fetched_ro...  25.1 us
    scatter-add x1, other arithmetic, on_device(): jax.ops.segment_sum(returned.reshape(-1, row_width), serve_rows.reshape(-...  24.1 us
  transfers between devices with their start and end apart: 7, of which 6 were waited for; matrix products, arithmetic and copies ran while one was open for 12% of the time, Pallas kernels for 0%

commit v1 on v0

v1 whole, which is shorter than its diff:
```python
import functools

import jax
import jax.numpy as jnp
from jax import lax
from jax.experimental import pallas as pl
from jax.experimental.pallas import tpu as pltpu
from jax.sharding import PartitionSpec as P

HEAD = 128
EPS = 1e-05
SCALE = HEAD**-0.5
MESH = pl.DeviceIdType.MESH
F32 = jnp.float32
BF16 = jnp.bfloat16
NN = (((1,), (0,)), ((), ()))
NT = (((1,), (1,)), ((), ()))
TN = (((0,), (0,)), ((), ()))


def dot(a, b, form=NN):
    return lax.dot_general(a, b, form, preferred_element_type=F32)


def iota(shape, dim):
    return lax.broadcasted_iota(jnp.int32, shape, dim)


def place(step, lane, side, sign):
    me = lax.axis_index("table")
    z, y, x = me // (side * side), (me // side) % side, me % side
    dz, dy, dx = lane, (step // side + lane) % side, (step + lane) % side
    if sign > 0:
        z, y, x = (z + dz) % side, (y + dy) % side, (x + dx) % side
    else:
        z, y, x = (z - dz + side) % side, (y - dy + side) % side, (x - dx + side) % side
    return (z * side + y) * side + x


def greet_all(side):
    barrier = pltpu.get_barrier_semaphore()
    core = lax.axis_index("ctx")

    def greet(step, lane):
        pl.semaphore_signal(
            barrier, inc=1, device_id=(place(step, lane, side, 1), core), device_id_type=MESH
        )

    for lane in range(1, side):
        greet(0, lane)

    @pl.loop(1, side * side)
    def _(step):
        for lane in range(side):
            greet(step, lane)


def exchange(send, recv, send_sem, recv_sem, step, lane, side, cap):
    row = pl.multiple_of((step * side + lane) * cap, cap)
    return pltpu.make_async_remote_copy(
        src_ref=send.at[pl.ds(row, cap)],
        dst_ref=recv.at[pl.ds(row, cap)],
        send_sem=send_sem.at[step * side + lane],
        recv_sem=recv_sem.at[step * side + lane],
        device_id=(place(step, lane, side, 1), lax.axis_index("ctx")),
        device_id_type=MESH,
    )


def for_steps(side, body):
    body(0, 1)

    @pl.loop(1, side * side)
    def _(step):
        body(step, 0)


def multi_hot(slots_ref, base, rows, columns):
    row = iota((rows, columns), 0) + base
    total = jnp.zeros((rows, columns), F32)
    for feature in range(slots_ref.shape[0]):
        total = total + jnp.where(slots_ref[pl.ds(feature, 1), :] == row, 1.0, 0.0)
    return total.astype(BF16)


def fetch_kernel(
    side, cap, table, serve, slots, out, rounded, picked, send, recv, hot, total, send_sem, recv_sem
):
    greet_all(side)
    lanes = side * cap
    table_rows = table.shape[0]
    rounded[...] = table[...].astype(BF16)
    square = iota((cap, cap), 0) == iota((cap, cap), 1)
    columns = iota((cap, table_rows), 1)

    def pick(step):
        for lane in range(side):
            ids = serve[pl.ds(place(step, lane, side, 1), 1), :]
            ids = jnp.sum(jnp.where(square, ids.astype(F32), 0.0), axis=1, keepdims=True)
            one_hot = jnp.where(ids.astype(jnp.int32) == columns, 1.0, 0.0)
            picked[lane * cap : (lane + 1) * cap, :] = one_hot.astype(BF16)
        row = pl.multiple_of(step * lanes, lanes)
        send[pl.ds(row, lanes), :] = dot(picked[...], rounded[...]).astype(BF16)

    pick(0)
    pl.semaphore_wait(pltpu.get_barrier_semaphore(), side**3 - 1)
    recv[0:cap, :] = send[0:cap, :]

    def start(step, first):
        for lane in range(first, side):
            exchange(send, recv, send_sem, recv_sem, step, lane, side, cap).start()

    start(0, 1)

    @pl.loop(1, side * side)
    def _(step):
        pick(step)
        start(step, 0)

    positions = slots.shape[1]

    @pl.loop(0, side * side)
    def _(step):
        for lane in range(side):
            base = place(step, lane, side, -1) * cap
            row = pl.multiple_of((step * side + lane) * cap, cap)
            hot[pl.ds(row, cap), :] = multi_hot(slots, base, cap, positions)

    total[...] = jnp.zeros_like(total)

    def take(step, first):
        for lane in range(first, side):
            exchange(send, recv, send_sem, recv_sem, step, lane, side, cap).wait_recv()
        row = pl.multiple_of(step * lanes, lanes)
        total[...] += dot(recv[pl.ds(row, lanes), :], hot[pl.ds(row, lanes), :], TN)

    for_steps(side, take)
    out[...] = total[...].T

    def sent(step, first):
        for lane in range(first, side):
            exchange(send, recv, send_sem, recv_sem, step, lane, side, cap).wait_send()

    for_steps(side, sent)


def fetch(side, item_table, serve_rows, slots):
    cap = serve_rows.shape[1]
    chips = side**3
    rows, width = item_table.shape
    positions = slots.shape[1]
    whole = pl.BlockSpec(memory_space=pltpu.VMEM)
    return pl.pallas_call(
        functools.partial(fetch_kernel, side, cap),
        out_shape=jax.ShapeDtypeStruct((positions, width), F32),
        in_specs=[whole] * 3,
        out_specs=whole,
        scratch_shapes=[
            pltpu.VMEM((rows, width), BF16),
            pltpu.VMEM((side * cap, rows), BF16),
            pltpu.VMEM((chips * cap, width), BF16),
            pltpu.VMEM((chips * cap, width), BF16),
            pltpu.VMEM((chips * cap, positions), BF16),
            pltpu.VMEM((width, positions), F32),
            pltpu.SemaphoreType.DMA((chips,)),
            pltpu.SemaphoreType.DMA((chips,)),
        ],
        compiler_params=pltpu.CompilerParams(
            collective_id=0, has_side_effects=True, vmem_limit_bytes=48 << 20
        ),
        name="fetch",
    )(item_table, serve_rows, slots)


def give_kernel(
    side, cap, grads, slots, serve, out,
    send, recv, total, half_send, half_recv, send_sem, recv_sem, half_sem,
):
    greet_all(side)
    table, core = lax.axis_index("table"), lax.axis_index("ctx")
    barrier = pltpu.get_barrier_semaphore()
    other = (table, 1 - core)
    pl.semaphore_signal(barrier, inc=1, device_id=other, device_id_type=MESH)
    lanes = side * cap
    positions = slots.shape[1]
    rows = total.shape[0]
    total[...] = jnp.zeros_like(total)

    def sums(step):
        for lane in range(side):
            base = place(step, lane, side, 1) * cap
            row = pl.multiple_of((step * side + lane) * cap, cap)
            send[pl.ds(row, cap), :] = dot(
                multi_hot(slots, base, cap, positions), grads[...]
            ).astype(BF16)

    sums(0)
    pl.semaphore_wait(barrier, side**3)
    recv[0:cap, :] = send[0:cap, :]

    def start(step, first):
        for lane in range(first, side):
            exchange(send, recv, send_sem, recv_sem, step, lane, side, cap).start()

    start(0, 1)

    @pl.loop(1, side * side)
    def _(step):
        sums(step)
        start(step, 0)

    def add(step, first):
        ids = [serve[pl.ds(place(step, lane, side, -1), 1), :] for lane in range(side)]
        one_hot = jnp.where(
            jnp.concatenate(ids, axis=1) == iota((rows, lanes), 0), 1.0, 0.0
        ).astype(BF16)
        for lane in range(first, side):
            exchange(send, recv, send_sem, recv_sem, step, lane, side, cap).wait_recv()
        row = pl.multiple_of(step * lanes, lanes)
        total[...] += dot(one_hot, recv[pl.ds(row, lanes), :])

    for_steps(side, add)
    half = rows // 2
    mine = pl.ds(pl.multiple_of(core * half, half), half)
    theirs = pl.ds(pl.multiple_of((1 - core) * half, half), half)
    half_send[...] = total[theirs, :].astype(BF16)
    swap = pltpu.make_async_remote_copy(
        src_ref=half_send,
        dst_ref=half_recv,
        send_sem=half_sem.at[0],
        recv_sem=half_sem.at[1],
        device_id=other,
        device_id_type=MESH,
    )
    swap.start()

    def sent(step, first):
        for lane in range(first, side):
            exchange(send, recv, send_sem, recv_sem, step, lane, side, cap).wait_send()

    for_steps(side, sent)
    swap.wait()
    out[...] = total[mine, :] + half_recv[...].astype(F32)


def give(side, grads, slots, serve_rows, rows):
    cap = serve_rows.shape[1]
    chips = side**3
    width = grads.shape[1]
    whole = pl.BlockSpec(memory_space=pltpu.VMEM)
    return pl.pallas_call(
        functools.partial(give_kernel, side, cap),
        out_shape=jax.ShapeDtypeStruct((rows // 2, width), F32),
        in_specs=[whole] * 3,
        out_specs=whole,
        scratch_shapes=[
            pltpu.VMEM((chips * cap, width), BF16),
            pltpu.VMEM((chips * cap, width), BF16),
            pltpu.VMEM((rows, width), F32),
            pltpu.VMEM((rows // 2, width), BF16),
            pltpu.VMEM((rows // 2, width), BF16),
            pltpu.SemaphoreType.DMA((chips,)),
            pltpu.SemaphoreType.DMA((chips,)),
            pltpu.SemaphoreType.DMA((2,)),
        ],
        compiler_params=pltpu.CompilerParams(
            collective_id=2, has_side_effects=True, vmem_limit_bytes=48 << 20
        ),
        name="give",
    )(grads, slots, serve_rows)


def layer_kernel(
    block, embedded, cotangent, lengths, w_proj, w_out, layer_out, grad_emb,
    x_all, g_all, weights_own, out_own, gate, value, query, keyrow, slope,
    grad_gated, attended, stat_send, stat_recv, soft, soft_slope, grad_att,
    grad_q, grad_k, grad_v, gated_own, gated_send, gated_recv, gx_own, gx_send, gx_recv,
    send_sem, recv_sem,
):
    table, core = lax.axis_index("table"), lax.axis_index("ctx")
    barrier = pltpu.get_barrier_semaphore()
    pl.semaphore_signal(barrier, inc=1, device_id=(table, 1 - core), device_id_type=MESH)
    rows, width = embedded.shape
    cols = value.shape[1]
    heads = cols // HEAD
    own_blocks = rows // block
    blocks = 2 * own_blocks
    length = lengths[0]

    def copy_over(src, dst, number):
        return pltpu.make_async_remote_copy(
            src_ref=src,
            dst_ref=dst,
            send_sem=send_sem.at[number],
            recv_sem=recv_sem.at[number],
            device_id=(table, 1 - core),
            device_id_type=MESH,
        )

    def rows_of(index):
        return pl.ds(pl.multiple_of(index * block, block), block)

    first = core * own_blocks
    start_cols = pl.multiple_of(core * cols, cols)

    def valid(index, height):
        return iota((height, 1), 0) + index * block < length

    def normalize(index):
        rows_x = embedded[rows_of(index), :]
        centred = rows_x - jnp.mean(rows_x, axis=-1, keepdims=True)
        inverse = lax.rsqrt(jnp.mean(centred * centred, axis=-1, keepdims=True) + EPS)
        return centred * inverse, inverse

    at_g, at_x = 0, own_blocks
    at_stat = 2 * own_blocks
    at_gated = at_stat + blocks
    at_gx = at_gated + own_blocks

    def send_x(index):
        here = rows_of(first + index)
        return copy_over(x_all.at[here], x_all.at[here], at_x + index)

    def send_g(index):
        here = rows_of(first + index)
        return copy_over(g_all.at[here], g_all.at[here], at_g + index)

    for index in range(own_blocks):
        x_all[rows_of(first + index), :] = normalize(index)[0].astype(BF16)
        if index == 0:
            pl.semaphore_wait(barrier, 1)
        send_x(index).start()
    for index in range(own_blocks):
        rows_g = cotangent[rows_of(index), :]
        g_all[rows_of(first + index), :] = jnp.where(
            valid(first + index, block), rows_g, jnp.zeros_like(rows_g)
        )
        send_g(index).start()
    for part in range(4):
        here = pl.multiple_of(part * 2 * cols + core * cols, cols)
        weights_own[part] = w_proj[:, pl.ds(here, cols)]
    out_own[...] = w_out[pl.ds(start_cols, cols), :]

    def project(index):
        here = rows_of(index)
        rows_x = x_all[here, :]
        for part, ref in enumerate((gate, value, query, keyrow)):
            h = dot(rows_x, weights_own[part]) * 0.5
            th = jnp.tanh(h)
            up = 1.0 + th
            act = h * up
            slope[here, part * cols : (part + 1) * cols] = 0.5 * (up + act * (1.0 - th))
            act = act.astype(BF16)
            if part == 1:
                act = jnp.where(valid(index, block), act, jnp.zeros_like(act))
            ref[here, :] = act

    def spread(index):
        here = rows_of(index)
        grad_gated[here, :] = dot(g_all[here, :], out_own[...], NT)

    @pl.loop(0, own_blocks)
    def _(index):
        project(first + index)
        spread(first + index)

    attended[...] = jnp.zeros_like(attended)
    grad_q[...] = jnp.zeros_like(grad_q)
    grad_k[...] = jnp.zeros_like(grad_k)
    grad_v[...] = jnp.zeros_like(grad_v)

    @pl.loop(0, own_blocks)
    def _(index):
        theirs = (1 - core) * own_blocks + index
        send_x(index).wait_recv()
        project(theirs)
        send_g(index).wait_recv()
        spread(theirs)

    def head(number):
        return slice(number * HEAD, (number + 1) * HEAD)

    def forward_pair(i, j, masked):
        slot = i % 2
        for number in range(heads):
            h = dot(query[rows_of(i), head(number)], keyrow[rows_of(j), head(number)], NT)
            h = h * (0.5 * SCALE)
            th = jnp.tanh(h)
            up = 1.0 + th
            act = h * up
            twice = up + act * (1.0 - th)
            if masked:
                allowed = iota((block, block), 1) <= iota((block, block), 0)
                act = jnp.where(allowed, act, 0.0)
                twice = jnp.where(allowed, twice, 0.0)
            act = act.astype(BF16)
            soft[slot, number, j] = act
            soft_slope[slot, number, j] = twice.astype(BF16)
            attended[rows_of(i), head(number)] += dot(act, value[rows_of(j), head(number)])

    def send_stat(i):
        return copy_over(stat_send.at[rows_of(i)], stat_recv.at[rows_of(i)], at_stat + i)

    def forward(i):
        @pl.loop(0, i)
        def _(j):
            forward_pair(i, j, False)

        forward_pair(i, i, True)
        here = rows_of(i)
        att = attended[here, :]
        t = grad_gated[here, :] * gate[here, :].astype(F32)
        lane = iota((block, 128), 1)
        sums = jnp.zeros((block, 128), F32)
        for number, term in enumerate((att, att * att, t, t * att)):
            sums = jnp.where(lane == number, jnp.sum(term, axis=1, keepdims=True), sums)
        stat_send[here, :] = sums
        send_stat(i).start()

    def is_own(i):
        return (i // own_blocks) == core

    def send_gated(index):
        here = rows_of(index)
        return copy_over(gated_send.at[here], gated_recv.at[here], at_gated + index)

    def send_gx(index):
        here = rows_of(index)
        return copy_over(gx_send.at[here], gx_recv.at[here], at_gx + index)

    def combine(i):
        here = rows_of(i)
        send_stat(i).wait_recv()
        mean = (stat_send[here, :] + stat_recv[here, :]) * (1.0 / (2 * cols))
        middle = mean[:, 0:1]
        inverse = lax.rsqrt(mean[:, 1:2] - middle * middle + EPS)
        mean_t = mean[:, 2:3]
        mean_tn = (mean[:, 3:4] - middle * mean_t) * inverse
        gates = gate[here, :].astype(F32)
        grads = grad_gated[here, :]
        normed = (attended[here, :] - middle) * inverse
        gated = (normed * gates).astype(BF16)
        grad_att[here, :] = ((grads * gates - mean_t - normed * mean_tn) * inverse).astype(BF16)
        grad_gated[here, :] = grads * normed
        local = rows_of(i % own_blocks)

        @pl.when(is_own(i))
        def _():
            gated_own[local, :] = gated

        @pl.when(jnp.logical_not(is_own(i)))
        def _():
            gated_send[local, :] = gated
            send_gated(i % own_blocks).start()

    def backward_pair(i, j):
        slot = i % 2
        for number in range(heads):
            at = head(number)
            grads = grad_att[rows_of(i), at]
            grad_p = dot(grads, value[rows_of(j), at], NT)
            grad_s = (grad_p * soft_slope[slot, number, j].astype(F32)).astype(BF16)
            grad_v[rows_of(j), at] += dot(soft[slot, number, j], grads, TN)
            grad_k[rows_of(j), at] += dot(grad_s, query[rows_of(i), at], TN)
            grad_q[rows_of(i), at] += dot(grad_s, keyrow[rows_of(j), at])

    def backward(i):
        combine(i)

        @pl.loop(0, i + 1)
        def _(j):
            backward_pair(i, j)

        here = rows_of(i)
        total = jnp.zeros((block, width), F32)
        for part in range(4):
            if part == 0:
                term = grad_gated[here, :]
            elif part == 1:
                term = jnp.where(valid(i, block), grad_v[here, :], 0.0)
            else:
                term = (grad_q, grad_k)[part - 2][here, :] * (0.5 * SCALE)
            term = (term * slope[here, part * cols : (part + 1) * cols]).astype(BF16)
            total = total + dot(term, weights_own[part], NT)
        local = rows_of(i % own_blocks)

        @pl.when(is_own(i))
        def _():
            gx_own[local, :] = total

        @pl.when(jnp.logical_not(is_own(i)))
        def _():
            gx_send[local, :] = total
            send_gx(i % own_blocks).start()

    forward(blocks - 1)

    @pl.loop(0, blocks - 1)
    def _(step):
        forward(blocks - 2 - step)
        backward(blocks - 1 - step)

    backward(0)

    for index in range(own_blocks):
        here = rows_of(index)
        send_gated(index).wait_recv()
        their_cols = pl.multiple_of((1 - core) * cols, cols)
        mixed = dot(gated_own[here, :], out_own[...]) + dot(
            gated_recv[here, :], w_out[pl.ds(their_cols, cols), :]
        )
        layer_out[here, :] = jnp.where(
            valid(first + index, block), embedded[here, :] + mixed, 0.0
        ).astype(BF16)
    for index in reversed(range(own_blocks)):
        here = rows_of(index)
        normal_x, inverse = normalize(index)
        send_gx(index).wait_recv()
        grad_x = gx_own[here, :] + gx_recv[here, :]
        middle = jnp.mean(grad_x, axis=-1, keepdims=True)
        along = jnp.mean(grad_x * normal_x, axis=-1, keepdims=True)
        masked = g_all[rows_of(first + index), :].astype(F32)
        grad_emb[here, :] = (masked + (grad_x - middle - normal_x * along) * inverse).astype(BF16)
    for index in range(own_blocks):
        send_x(index).wait_send()
        send_g(index).wait_send()
        send_gated(index).wait_send()
        send_gx(index).wait_send()

    @pl.loop(0, blocks)
    def _(i):
        send_stat(i).wait_send()


def layer(embedded, cotangent, lengths, w_proj, w_out, block):
    rows, width = embedded.shape
    total = 2 * rows
    cols = w_out.shape[0] // 2
    heads = cols // HEAD
    own_blocks = rows // block
    blocks = 2 * own_blocks
    copies = 4 * own_blocks + blocks
    whole = pl.BlockSpec(memory_space=pltpu.VMEM)
    wide_b, wide_f = pltpu.VMEM((total, cols), BF16), pltpu.VMEM((total, cols), F32)
    pairs = pltpu.VMEM((2, heads, blocks, block, block), BF16)
    return pl.pallas_call(
        functools.partial(layer_kernel, block),
        out_shape=(
            jax.ShapeDtypeStruct((rows, width), BF16),
            jax.ShapeDtypeStruct((rows, width), BF16),
        ),
        in_specs=[whole, whole, pl.BlockSpec(memory_space=pltpu.SMEM), whole, whole],
        out_specs=(whole, whole),
        scratch_shapes=[
            pltpu.VMEM((total, width), BF16),
            pltpu.VMEM((total, width), BF16),
            pltpu.VMEM((4, width, cols), BF16),
            pltpu.VMEM((cols, width), BF16),
            wide_b,
            wide_b,
            wide_b,
            wide_b,
            pltpu.VMEM((total, 4 * cols), F32),
            wide_f,
            wide_f,
            pltpu.VMEM((total, 128), F32),
            pltpu.VMEM((total, 128), F32),
            pairs,
            pairs,
            wide_b,
            wide_f,
            wide_f,
            wide_f,
            pltpu.VMEM((rows, cols), BF16),
            pltpu.VMEM((rows, cols), BF16),
            pltpu.VMEM((rows, cols), BF16),
            pltpu.VMEM((rows, width), F32),
            pltpu.VMEM((rows, width), F32),
            pltpu.VMEM((rows, width), F32),
            pltpu.SemaphoreType.DMA((copies,)),
            pltpu.SemaphoreType.DMA((copies,)),
        ],
        compiler_params=pltpu.CompilerParams(
            collective_id=1, has_side_effects=True, vmem_limit_bytes=62 << 20
        ),
        name="layer",
    )(embedded, cotangent, lengths, w_proj, w_out)


def on_device(side, item_table, serve_rows, token_slots, lengths, w_proj, w_out, grad_out):
    slots = token_slots[0].T
    embedded = fetch(side, item_table, serve_rows, slots)
    layer_out, grad_emb = layer(
        embedded, grad_out[0], lengths, w_proj, w_out, min(512, embedded.shape[0])
    )
    grad_table = give(side, grad_emb, slots, serve_rows, item_table.shape[0])
    return (layer_out[None], grad_table)


def solution(mesh):
    placed = (
        P("table", None),
        P("table", "ctx"),
        P("table", "ctx", None),
        P("table"),
        P(),
        P(),
        P("table", "ctx", None),
    )
    side = round(mesh.shape["table"] ** (1 / 3))
    return jax.shard_map(
        functools.partial(on_device, side),
        mesh=mesh,
        in_specs=placed,
        out_specs=(P("table", "ctx", None), P(("table", "ctx"), None)),
        check_vma=False,
    )
```

time: 605 us -> 128 us (0.21); the launches traced: 598 us -> 128 us
  matrix products: 176 us -> 0 us
  other arithmetic: 138 us -> 0 us
  waiting for transfers between devices: 127 us -> 0 us
  Pallas kernels: 0 us -> 118 us
  local copies, waits for them, and re-layouts: 118 us -> 7.9 us
  starting transfers between devices: 23.3 us -> 0 us
  between operations: 15.1 us -> 1.35 us
    dot_general x28 -> x0, matrix products: 176 us -> none  [the longest x4 40.4 us: key_terms(): jnp.einsum('hij,ihd->jhd', grad_scores, split_heads(query_block), preferr...]
    pallas_call x0 -> x3, Pallas kernels: none -> 118 us  [the longest x1 40.7 us: layer(): pl.pallas_call(functools.partial(layer_kernel, block), out_shape=(jax.Sha...]
    all_to_all x2 -> x0, waiting for transfers between devices: 82.7 us -> none  [the longest x1 53.5 us: on_device(): lax.all_to_all(served, 'table', split_axis=0, concat_axis=0, tiled=True)]
    scatter-add x2 -> x0, other arithmetic: 49.2 us -> none  [the longest x1 25.1 us: on_device(): jax.ops.segment_sum(spread, slot_ids.reshape(-1), num_segments=fetched_ro...]
    add x29 -> x0, other arithmetic: 42.5 us -> none  [the longest x4 22.5 us: both_sides(): grad_v_now = current[2] + more_v]
    gather x5 -> x0, local copies, waits for them, and re-layouts: 41.3 us -> none  [the longest x3 18.2 us: on_device(): embedded = embedded + fetched_rows[slot_ids[:, feature]]]
    all_gather x4 -> x0, waiting for transfers between devices: 37.6 us -> none  [the longest x1 13.6 us: on_device(): lax.all_gather(grad_attended, 'ctx', axis=0, tiled=True)]
    dynamic_slice x32 -> x0, local copies, waits for them, and re-layouts: 28.9 us -> none  [visit_block(): lax.dynamic_slice_in_dim(one_piece, offset, block_rows, 0)]
  transfers between devices with their start and end apart: 7 -> 0, of which waited for: 6 -> 0; matrix products, arithmetic and copies ran while one was open for 12% -> 0% of each run, Pallas kernels for 0% -> 0%
where the time goes in v1:
time: 128 us
  Pallas kernels  118 us (92%)
  local copies, waits for them, and re-layouts  7.9 us (6%)
  between operations  1.35 us (1%)
    pallas_call x1, Pallas kernels, layer(): pl.pallas_call(functools.partial(layer_kernel, block), out_shape=(jax.Sha...  40.7 us
    pallas_call x1, Pallas kernels, give(): pl.pallas_call(functools.partial(give_kernel, side, cap), out_shape=jax.S...  39.9 us
    pallas_call x1, Pallas kernels, fetch(): pl.pallas_call(functools.partial(fetch_kernel, side, cap), out_shape=jax....  37.7 us
    unnamed x16, local copies, waits for them, and re-layouts  7.9 us

profile of v1, /device:TPU:1, one launch (start us, length us, event | category | flops | bytes accessed | tf_op | source)
XLA Modules:
  0.0 127.5 jit_solution(14007151410114565184)
XLA Ops:
  1.3 0.0 copy-start.1
  1.3 1.6 %copy-done.1 = f32[2048,256]{1,0:T(8,128)S(1)} copy-done((f32[2048,256]{1,0:T(8,128)S(1)}, f32[2048,256]{1,0:T(8,128)}, u32[]{:S(2)}) %copy-start.1) | copy-done | bytes 2097176
  2.9 0.0 copy-start.3
  2.9 0.8 copy-done.3
  3.6 0.0 copy-start.5
  3.6 0.7 copy-done.5
  4.3 37.7 %fetch.1.embedded = f32[1024,256]{1,0:T(8,128)S(1)} custom-call(f32[2048,256]{1,0:T(8,128)S(1)} %copy-done.1, s32[64,64]{1,0:T(8,128)S(1)} %copy-done.3, s32[4,1024]{1,0:T(4,128)S(1)} %bitcast.5), custom_call_target="tpu_custom_call" | custom-call | tf_op jit(solution)/shard_map/fetch/pallas_call | solution.py:153
  42.0 0.0 copy-start
  42.1 1.0 copy-done
  43.0 0.0 copy-start.4
  43.0 0.0 copy-start.6
  43.0 40.7 %layer.1 = (bf16[1024,256]{1,0:T(8,128)(2,1)}, bf16[1024,256]{1,0:T(8,128)(2,1)}) custom-call(f32[1024,256]{1,0:T(8,128)} %copy-done, bf16[1024,256]{1,0:T(8,128)(2,1)} %bitcast.8, s32[1]{0:T(128)S(6)} %copy.11.lengths, bf16[256,2048]{1,0:T(8,128)(2,1)} %w_proj.1, bf16[512,256]{1,0:T(8,128)(2,1)} %w_out.1), custom_call_target="tpu_custom_call" | custom-call | tf_op jit(solution)/shard_map/layer/pallas_call | solution.py:546
  83.7 0.0 copy-done.4
  83.7 0.0 copy-done.6
  83.7 0.0 copy-start.2
  83.7 1.0 copy-done.2
  84.8 39.9 %give.1 = f32[1024,256]{1,0:T(8,128)S(1)} custom-call(bf16[1024,256]{1,0:T(8,128)(2,1)S(1)} %copy-done.2, s32[4,1024]{1,0:T(4,128)S(1)} %bitcast.6, s32[64,64]{1,0:T(8,128)S(1)} %copy-done.4), custom_call_target="tpu_custom_call" | custom-call | tf_op jit(solution)/shard_map/give/pallas_call | solution.py:251
  124.7 1.9 %copy.12 = bf16[1,1024,256]{2,1,0:T(8,128)(2,1)} copy(bf16[1,1024,256]{2,1,0:T(8,128)(2,1)} %bitcast.7) | data formatting | bytes 1048576
  126.6 1.0 copy.13
Async XLA Ops:
  1.3 1.6 %copy-start.1 = (f32[2048,256]{1,0:T(8,128)S(1)}, f32[2048,256]{1,0:T(8,128)}, u32[]{:S(2)}) copy-start(f32[2048,256]{1,0:T(8,128)} %table.1) | copy-start | bytes 6291460
  2.9 0.8 copy-start.3
  3.6 0.7 copy-start.5
  42.0 1.0 copy-start
  43.0 40.7 %copy-start.4 = (s32[64,64]{1,0:T(8,128)S(1)}, s32[64,64]{1,0:T(8,128)}, u32[]{:S(2)}) copy-start(s32[64,64]{1,0:T(8,128)} %serve.3) | copy-start | bytes 49156
  43.0 40.7 %copy-start.6 = (s32[1,1024,4]{1,2,0:T(4,128)S(1)}, s32[1,1024,4]{1,2,0:T(4,128)}, u32[]{:S(2)}) copy-start(s32[1,1024,4]{1,2,0:T(4,128)} %param.9) | copy-start | bytes 49156
  83.7 1.0 copy-start.2

commit v2 on v1

v2 whole, which is shorter than its diff:
```python
import functools

import jax
import jax.numpy as jnp
from jax import lax
from jax.experimental import pallas as pl
from jax.experimental.pallas import tpu as pltpu
from jax.sharding import PartitionSpec as P

HEAD = 128
EPS = 1e-05
SCALE = HEAD**-0.5
MESH = pl.DeviceIdType.MESH
F32 = jnp.float32
BF16 = jnp.bfloat16
NN = (((1,), (0,)), ((), ()))
NT = (((1,), (1,)), ((), ()))
TN = (((0,), (0,)), ((), ()))


def dot(a, b, form=NN):
    return lax.dot_general(a, b, form, preferred_element_type=F32)


def iota(shape, dim):
    return lax.broadcasted_iota(jnp.int32, shape, dim)


def place(step, lane, side, sign):
    me = lax.axis_index("table")
    z, y, x = me // (side * side), (me // side) % side, me % side
    dz, dy, dx = lane, (step // side + lane) % side, (step + lane) % side
    if sign > 0:
        z, y, x = (z + dz) % side, (y + dy) % side, (x + dx) % side
    else:
        z, y, x = (z - dz + side) % side, (y - dy + side) % side, (x - dx + side) % side
    return (z * side + y) * side + x


def greet_all(side):
    barrier = pltpu.get_barrier_semaphore()
    core = lax.axis_index("ctx")

    def greet(step, lane):
        pl.semaphore_signal(
            barrier, inc=1, device_id=(place(step, lane, side, 1), core), device_id_type=MESH
        )

    for lane in range(1, side):
        greet(0, lane)

    @pl.loop(1, side * side)
    def _(step):
        for lane in range(side):
            greet(step, lane)


def exchange(side, cap, send, recv, send_sem, recv_sem, step, lane):
    row = pl.multiple_of((step * side + lane) * cap, cap)
    return pltpu.make_async_remote_copy(
        src_ref=send.at[pl.ds(row, cap)],
        dst_ref=recv.at[pl.ds(row, cap)],
        send_sem=send_sem.at[step * side + lane],
        recv_sem=recv_sem.at[step * side + lane],
        device_id=(place(step, lane, side, 1), lax.axis_index("ctx")),
        device_id_type=MESH,
    )


def for_steps(side, body):
    body(0, 1)

    @pl.loop(1, side * side)
    def _(step):
        body(step, 0)


def multi_hot(slots_ref, base, rows, start, columns):
    row = iota((rows, columns), 0) + base
    total = jnp.zeros((rows, columns), F32)
    for feature in range(slots_ref.shape[0]):
        total = total + jnp.where(slots_ref[feature : feature + 1, start : start + columns] == row, 1.0, 0.0)
    return total.astype(BF16)


def kernel(
    side, cap, block,
    table_in, serve_in, slots_in, lengths, w_proj_in, w_out_in, cotangent_in,
    layer_out, grad_table,
    serve, slots, weights_own, w_out, cotangent, picked, send, recv, back, turned, embedded,
    x_all, g_all, gate, value, query, keyrow, slope, grad_gated, attended, stat_send, stat_recv,
    soft, soft_slope, grad_att, grad_q, grad_k, grad_v, gated_own, gated_send, gated_recv,
    gx_own, gx_send, gx_recv, grads, half_send, half_recv, result,
    load_sem, store_sem, out_sem, in_sem, back_out_sem, back_in_sem, core_out_sem, core_in_sem,
):
    table, core = lax.axis_index("table"), lax.axis_index("ctx")
    other = (table, 1 - core)
    barrier = pltpu.get_barrier_semaphore()
    steps = side * side
    lanes = side * cap
    table_rows, width = grad_k.shape
    positions = slots.shape[1]
    cols = value.shape[1]
    heads = cols // HEAD
    own_blocks = positions // block
    blocks = 2 * own_blocks
    first = core * own_blocks
    length = lengths[0]
    own_cols = pl.multiple_of(core * cols, cols)
    their_cols = pl.multiple_of((1 - core) * cols, cols)

    loads = [(serve_in, serve), (table_in, grad_k), (slots_in, slots), (cotangent_in, cotangent)]
    for part in range(4):
        here = pl.multiple_of(part * 2 * cols + core * cols, cols)
        loads.append((w_proj_in.at[:, pl.ds(here, cols)], weights_own.at[part]))
    loads.append((w_out_in, w_out))
    loads = [
        pltpu.make_async_copy(src, dst, load_sem.at[number])
        for number, (src, dst) in enumerate(loads)
    ]
    for load in loads:
        load.start()
    greet_all(side)
    pl.semaphore_signal(barrier, inc=1, device_id=other, device_id_type=MESH)

    rounded = keyrow
    loads[0].wait()
    loads[1].wait()
    rounded[...] = grad_k[...].astype(BF16)
    square = iota((cap, cap), 0) == iota((cap, cap), 1)
    columns = iota((cap, table_rows), 1)

    def pick(step):
        for lane in range(side):
            ids = serve[pl.ds(place(step, lane, side, 1), 1), :]
            ids = jnp.sum(jnp.where(square, ids.astype(F32), 0.0), axis=1, keepdims=True)
            one_hot = jnp.where(ids.astype(jnp.int32) == columns, 1.0, 0.0)
            picked[lane * cap : (lane + 1) * cap, :] = one_hot.astype(BF16)
        row = pl.multiple_of(step * lanes, lanes)
        send[pl.ds(row, lanes), :] = dot(picked[...], rounded[...]).astype(BF16)

    ask = functools.partial(exchange, side, cap, send, recv, out_sem, in_sem)

    def start_ask(step, first_lane):
        for lane in range(first_lane, side):
            ask(step, lane).start()

    pick(0)
    pl.semaphore_wait(barrier, side**3)
    recv[0:cap, :] = send[0:cap, :]
    start_ask(0, 1)

    @pl.loop(1, steps)
    def _(step):
        pick(step)
        start_ask(step, 0)

    for load in loads[2:]:
        load.wait()

    def rows_of(index):
        return pl.ds(pl.multiple_of(index * block, block), block)

    def valid(index, height):
        return iota((height, 1), 0) + index * block < length

    def copy_over(src, dst, number):
        return pltpu.make_async_remote_copy(
            src_ref=src,
            dst_ref=dst,
            send_sem=core_out_sem.at[number],
            recv_sem=core_in_sem.at[number],
            device_id=other,
            device_id_type=MESH,
        )

    at_g, at_x = 0, own_blocks
    at_stat = 2 * own_blocks
    at_gated = at_stat + blocks
    at_gx = at_gated + own_blocks
    at_half = at_gx + own_blocks

    def send_x(index):
        here = rows_of(first + index)
        return copy_over(x_all.at[here], x_all.at[here], at_x + index)

    def send_g(index):
        here = rows_of(first + index)
        return copy_over(g_all.at[here], g_all.at[here], at_g + index)

    for index in range(own_blocks):
        rows_g = cotangent[rows_of(index), :]
        g_all[rows_of(first + index), :] = jnp.where(
            valid(first + index, block), rows_g, jnp.zeros_like(rows_g)
        )
        send_g(index).start()
    grad_k[...] = jnp.zeros_like(grad_k)
    grad_v[...] = jnp.zeros_like(grad_v)
    turned[...] = jnp.zeros_like(turned)

    def hot_rows(index, row, count):
        return pl.ds(pl.multiple_of(index * steps * lanes + row, cap), count)

    @pl.loop(0, steps)
    def _(step):
        for lane in range(side):
            base = place(step, lane, side, -1) * cap
            row = pl.multiple_of((step * side + lane) * cap, cap)
            for index in range(own_blocks):
                soft[hot_rows(index, row, cap), :] = multi_hot(slots, base, cap, index * block, block)

    for index in range(own_blocks):
        send_g(index).wait_recv()

    def take(step, first_lane):
        for lane in range(first_lane, side):
            ask(step, lane).wait_recv()
        row = pl.multiple_of(step * lanes, lanes)
        for index in range(own_blocks):
            turned[:, index * block : (index + 1) * block] += dot(
                recv[pl.ds(row, lanes), :], soft[hot_rows(index, row, lanes), :], TN
            )

    for_steps(side, take)
    embedded[...] = turned[...].T

    def normalize(index):
        rows_x = embedded[rows_of(index), :]
        centred = rows_x - jnp.mean(rows_x, axis=-1, keepdims=True)
        inverse = lax.rsqrt(jnp.mean(centred * centred, axis=-1, keepdims=True) + EPS)
        return centred * inverse, inverse

    for index in range(own_blocks):
        x_all[rows_of(first + index), :] = normalize(index)[0].astype(BF16)
        send_x(index).start()

    def project(index):
        here = rows_of(index)
        rows_x = x_all[here, :]
        for part, ref in enumerate((gate, value, query, keyrow)):
            h = dot(rows_x, weights_own[part]) * 0.5
            th = jnp.tanh(h)
            up = 1.0 + th
            act = h * up
            slope[here, part * cols : (part + 1) * cols] = (
                0.5 * (up + act * (1.0 - th))
            ).astype(BF16)
            act = act.astype(BF16)
            if part == 1:
                act = jnp.where(valid(index, block), act, jnp.zeros_like(act))
            ref[here, :] = act

    @pl.loop(0, own_blocks)
    def _(index):
        project(first + index)

    @pl.loop(0, own_blocks)
    def _(index):
        send_x(index).wait_recv()
        project((1 - core) * own_blocks + index)

    def head(number):
        return slice(number * HEAD, (number + 1) * HEAD)

    def pair_ref(ref, i, number, j):
        row = (((i % 2) * heads + number) * blocks + j) * block
        return ref.at[pl.ds(pl.multiple_of(row, block), block)]

    def forward_pair(i, j, masked):
        for number in range(heads):
            h = dot(query[rows_of(i), head(number)], keyrow[rows_of(j), head(number)], NT)
            h = h * (0.5 * SCALE)
            th = jnp.tanh(h)
            up = 1.0 + th
            act = h * up
            twice = up + act * (1.0 - th)
            if masked:
                allowed = iota((block, block), 1) <= iota((block, block), 0)
                act = jnp.where(allowed, act, 0.0)
                twice = jnp.where(allowed, twice, 0.0)
            act = act.astype(BF16)
            pair_ref(soft, i, number, j)[...] = act
            pair_ref(soft_slope, i, number, j)[...] = twice.astype(BF16)
            added = dot(act, value[rows_of(j), head(number)])
            if masked:
                attended[i % 2, :, head(number)] = added
            else:
                attended[i % 2, :, head(number)] += added

    def send_stat(i):
        return copy_over(stat_send.at[rows_of(i)], stat_recv.at[rows_of(i)], at_stat + i)

    def forward(i):
        forward_pair(i, i, True)
        here = rows_of(i)
        grad_gated[i % 2] = dot(g_all[here, :], w_out[pl.ds(own_cols, cols), :], NT)

        @pl.loop(0, i)
        def _(j):
            forward_pair(i, j, False)

        att = attended[i % 2]
        t = grad_gated[i % 2] * gate[here, :].astype(F32)
        lane = iota((block, 128), 1)
        sums = jnp.zeros((block, 128), F32)
        for number, term in enumerate((att, att * att, t, t * att)):
            sums = jnp.where(lane == number, jnp.sum(term, axis=1, keepdims=True), sums)
        stat_send[here, :] = sums
        send_stat(i).start()

    def is_own(i):
        return (i // own_blocks) == core

    def send_gated(index):
        here = rows_of(index)
        return copy_over(gated_send.at[here], gated_recv.at[here], at_gated + index)

    def send_gx(index):
        here = rows_of(index)
        return copy_over(gx_send.at[here], gx_recv.at[here], at_gx + index)

    def combine(i):
        here = rows_of(i)
        send_stat(i).wait_recv()
        mean = (stat_send[here, :] + stat_recv[here, :]) * (1.0 / (2 * cols))
        middle = mean[:, 0:1]
        inverse = lax.rsqrt(mean[:, 1:2] - middle * middle + EPS)
        mean_t = mean[:, 2:3]
        mean_tn = (mean[:, 3:4] - middle * mean_t) * inverse
        gates = gate[here, :].astype(F32)
        grad_rows = grad_gated[i % 2]
        normed = (attended[i % 2] - middle) * inverse
        gated = (normed * gates).astype(BF16)
        grad_att[...] = ((grad_rows * gates - mean_t - normed * mean_tn) * inverse).astype(BF16)
        grad_gated[i % 2] = grad_rows * normed
        local = rows_of(i % own_blocks)

        @pl.when(is_own(i))
        def _():
            gated_own[local, :] = gated

        @pl.when(jnp.logical_not(is_own(i)))
        def _():
            gated_send[local, :] = gated
            send_gated(i % own_blocks).start()

    def backward_pair(i, j):
        for number in range(heads):
            at = head(number)
            grad_rows = grad_att[:, at]
            grad_p = dot(grad_rows, value[rows_of(j), at], NT)
            twice = pair_ref(soft_slope, i, number, j)[...]
            grad_s = (grad_p * twice.astype(F32)).astype(BF16)
            grad_v[rows_of(j), at] += dot(pair_ref(soft, i, number, j)[...], grad_rows, TN)
            grad_k[rows_of(j), at] += dot(grad_s, query[rows_of(i), at], TN)
            grad_q[:, at] += dot(grad_s, keyrow[rows_of(j), at])

    def backward(i):
        combine(i)
        grad_q[...] = jnp.zeros_like(grad_q)

        @pl.loop(0, i + 1)
        def _(j):
            backward_pair(i, j)

        here = rows_of(i)
        total = jnp.zeros((block, width), F32)
        for part in range(4):
            if part == 0:
                term = grad_gated[i % 2]
            elif part == 1:
                term = jnp.where(valid(i, block), grad_v[here, :], 0.0)
            elif part == 2:
                term = grad_q[...] * (0.5 * SCALE)
            else:
                term = grad_k[here, :] * (0.5 * SCALE)
            slopes = slope[here, part * cols : (part + 1) * cols].astype(F32)
            total = total + dot((term * slopes).astype(BF16), weights_own[part], NT)
        local = rows_of(i % own_blocks)

        @pl.when(is_own(i))
        def _():
            gx_own[local, :] = total

        @pl.when(jnp.logical_not(is_own(i)))
        def _():
            gx_send[local, :] = total
            send_gx(i % own_blocks).start()

    forward(blocks - 1)

    @pl.loop(0, blocks - 1)
    def _(step):
        forward(blocks - 2 - step)
        backward(blocks - 1 - step)

    backward(0)

    def mix(index):
        here = rows_of(index)
        send_gated(index).wait_recv()
        mixed = dot(gated_own[here, :], w_out[pl.ds(own_cols, cols), :]) + dot(
            gated_recv[here, :], w_out[pl.ds(their_cols, cols), :]
        )
        cotangent[here, :] = jnp.where(
            valid(first + index, block), embedded[here, :] + mixed, 0.0
        ).astype(BF16)

    for index in reversed(range(own_blocks)):
        here = rows_of(index)
        normal_x, inverse = normalize(index)
        send_gx(index).wait_recv()
        grad_x = gx_own[here, :] + gx_recv[here, :]
        middle = jnp.mean(grad_x, axis=-1, keepdims=True)
        along = jnp.mean(grad_x * normal_x, axis=-1, keepdims=True)
        masked = g_all[rows_of(first + index), :].astype(F32)
        grads[here, :] = (masked + (grad_x - middle - normal_x * along) * inverse).astype(BF16)

    def sent(step, first_lane):
        for lane in range(first_lane, side):
            ask(step, lane).wait_send()

    for_steps(side, sent)
    give = functools.partial(exchange, side, cap, send, back, back_out_sem, back_in_sem)

    def sums_back(step):
        for lane in range(side):
            base = place(step, lane, side, 1) * cap
            row = pl.multiple_of((step * side + lane) * cap, cap)
            send[pl.ds(row, cap), :] = dot(
                multi_hot(slots, base, cap, 0, positions), grads[...]
            ).astype(BF16)

    def start_give(step, first_lane):
        for lane in range(first_lane, side):
            give(step, lane).start()

    sums_back(0)
    back[0:cap, :] = send[0:cap, :]
    start_give(0, 1)

    @pl.loop(1, steps)
    def _(step):
        sums_back(step)
        start_give(step, 0)

    for index in range(own_blocks):
        mix(index)
    store = pltpu.make_async_copy(cotangent, layer_out, store_sem.at[0])
    store.start()
    total = grad_k
    total[...] = jnp.zeros_like(total)

    def add(step, first_lane):
        ids = [serve[pl.ds(place(step, lane, side, -1), 1), :] for lane in range(side)]
        one_hot = jnp.where(
            jnp.concatenate(ids, axis=1) == iota((table_rows, lanes), 0), 1.0, 0.0
        ).astype(BF16)
        for lane in range(first_lane, side):
            give(step, lane).wait_recv()
        row = pl.multiple_of(step * lanes, lanes)
        total[...] += dot(one_hot, back[pl.ds(row, lanes), :])

    for_steps(side, add)
    half = table_rows // 2
    mine = pl.ds(pl.multiple_of(core * half, half), half)
    theirs = pl.ds(pl.multiple_of((1 - core) * half, half), half)
    half_send[...] = total[theirs, :].astype(BF16)
    swap = copy_over(half_send, half_recv, at_half)
    swap.start()

    def given(step, first_lane):
        for lane in range(first_lane, side):
            give(step, lane).wait_send()

    for_steps(side, given)
    for index in range(own_blocks):
        send_x(index).wait_send()
        send_g(index).wait_send()
        send_gated(index).wait_send()
        send_gx(index).wait_send()

    @pl.loop(0, blocks)
    def _(i):
        send_stat(i).wait_send()

    swap.wait()
    result[...] = total[mine, :] + half_recv[...].astype(F32)
    last = pltpu.make_async_copy(result, grad_table, store_sem.at[1])
    last.start()
    store.wait()
    last.wait()


def on_device(side, item_table, serve_rows, token_slots, lengths, w_proj, w_out, grad_out):
    slots = token_slots[0].T
    cap = serve_rows.shape[1]
    chips = side**3
    table_rows, width = item_table.shape
    positions = slots.shape[1]
    block = min(512, positions)
    total = 2 * positions
    cols = w_out.shape[0] // 2
    heads = cols // HEAD
    own_blocks = positions // block
    blocks = 2 * own_blocks
    copies = 4 * own_blocks + blocks + 1
    anywhere = pl.BlockSpec(memory_space=pl.ANY)
    sems = pltpu.SemaphoreType.DMA

    def rows_b(rows, columns):
        return pltpu.VMEM((rows, columns), BF16)

    def rows_f(rows, columns):
        return pltpu.VMEM((rows, columns), F32)

    pairs = rows_b(2 * heads * blocks * block, block)
    scratch = {
        "serve": pltpu.VMEM(serve_rows.shape, jnp.int32),
        "slots": pltpu.VMEM(slots.shape, jnp.int32),
        "weights_own": pltpu.VMEM((4, width, cols), BF16),
        "w_out": pltpu.VMEM(w_out.shape, BF16),
        "cotangent": rows_b(positions, width),
        "picked": rows_b(side * cap, table_rows),
        "send": rows_b(chips * cap, width),
        "recv": rows_b(chips * cap, width),
        "back": rows_b(chips * cap, width),
        "turned": rows_f(width, positions),
        "embedded": rows_f(positions, width),
        "x_all": rows_b(total, width),
        "g_all": rows_b(total, width),
        "gate": rows_b(total, cols),
        "value": rows_b(total, cols),
        "query": rows_b(total, cols),
        "keyrow": rows_b(total, cols),
        "slope": rows_b(total, 4 * cols),
        "grad_gated": pltpu.VMEM((2, block, cols), F32),
        "attended": pltpu.VMEM((2, block, cols), F32),
        "stat_send": rows_f(total, 128),
        "stat_recv": rows_f(total, 128),
        "soft": pairs,
        "soft_slope": pairs,
        "grad_att": rows_b(block, cols),
        "grad_q": rows_f(block, cols),
        "grad_k": rows_f(total, cols),
        "grad_v": rows_f(total, cols),
        "gated_own": rows_b(positions, cols),
        "gated_send": rows_b(positions, cols),
        "gated_recv": rows_b(positions, cols),
        "gx_own": rows_f(positions, width),
        "gx_send": rows_f(positions, width),
        "gx_recv": rows_f(positions, width),
        "grads": rows_b(positions, width),
        "half_send": rows_b(table_rows // 2, width),
        "half_recv": rows_b(table_rows // 2, width),
        "result": rows_f(table_rows // 2, width),
        "load_sem": sems((9,)),
        "store_sem": sems((2,)),
        "out_sem": sems((chips,)),
        "in_sem": sems((chips,)),
        "back_out_sem": sems((chips,)),
        "back_in_sem": sems((chips,)),
        "core_out_sem": sems((copies,)),
        "core_in_sem": sems((copies,)),
    }
    layer_out, grad_table = pl.pallas_call(
        functools.partial(kernel, side, cap, block),
        out_shape=(
            jax.ShapeDtypeStruct((positions, width), BF16),
            jax.ShapeDtypeStruct((table_rows // 2, width), F32),
        ),
        in_specs=[anywhere] * 3 + [pl.BlockSpec(memory_space=pltpu.SMEM)] + [anywhere] * 3,
        out_specs=(anywhere, anywhere),
        scratch_shapes=list(scratch.values()),
        compiler_params=pltpu.CompilerParams(
            collective_id=0, has_side_effects=True, vmem_limit_bytes=63 << 20
        ),
        name="hstu",
    )(item_table, serve_rows, slots, lengths, w_proj, w_out, grad_out[0])
    return (layer_out[None], grad_table)


def solution(mesh):
    placed = (
        P("table", None),
        P("table", "ctx"),
        P("table", "ctx", None),
        P("table"),
        P(),
        P(),
        P("table", "ctx", None),
    )
    side = round(mesh.shape["table"] ** (1 / 3))
    return jax.shard_map(
        functools.partial(on_device, side),
        mesh=mesh,
        in_specs=placed,
        out_specs=(P("table", "ctx", None), P(("table", "ctx"), None)),
        check_vma=False,
    )
```

time: 128 us -> 117 us (0.914)
  Pallas kernels: 118 us -> 111 us
  local copies, waits for them, and re-layouts: 7.9 us -> 4.13 us
    pallas_call x3 -> x1, Pallas kernels: 118 us -> 111 us  [on_device(): pl.pallas_call(functools.partial(kernel, side, cap, block), out_shape=(ja...]
    unnamed x16 -> x2, local copies, waits for them, and re-layouts: 7.9 us -> 4.13 us
where the time goes in v2:
time: 117 us
  Pallas kernels  111 us (95%)
  local copies, waits for them, and re-layouts  4.13 us (4%)
  between operations  1.29 us (1%)
    pallas_call x1, Pallas kernels, on_device(): pl.pallas_call(functools.partial(kernel, side, cap, block), out_shape=(ja...  111 us
    unnamed x2, local copies, waits for them, and re-layouts  4.13 us

profile of v2, /device:TPU:1, one launch (start us, length us, event | category | flops | bytes accessed | tf_op | source)
XLA Modules:
  0.0 116.6 jit_solution(6088216516137883128)
XLA Ops:
  1.3 111.2 %hstu.1 = (bf16[1024,256]{1,0:T(8,128)(2,1)}, f32[1024,256]{1,0:T(8,128)}) custom-call(f32[2048,256]{1,0:T(8,128)} %table_in.1, s32[64,64]{1,0:T(8,128)} %serve_in.1, s32[4,1024]{1,0:T(4,128)} %bitcast.7, s32[1]{0:T(128)S(6)} %copy.11.lengths, bf16[256,2048]{1,0:T(8,128)(2,1)} %w_proj_in.1, bf16[512,256]{1,0:T(8,128)(2,1)} %w_out_in.1, bf16[1024,256]{1,0:T(8,128)(2,1)} %bitcast.5), custom_call_target="tpu_custom_call" | custom-call | tf_op jit(solution)/shard_map/hstu/pallas_call | solution.py:566
  112.4 1.9 %copy.12 = bf16[1,1024,256]{2,1,0:T(8,128)(2,1)} copy(bf16[1,1024,256]{2,1,0:T(8,128)(2,1)} %bitcast.6) | data formatting | bytes 1048576
  114.3 2.3 %copy.13 = f32[1024,256]{1,0:T(8,128)} copy(f32[1024,256]{1,0:T(8,128)} %get-tuple-element.9) | data formatting | bytes 2097152

commit v3 on v2

--- a/solution.py
+++ b/solution.py
@@ -28,13 +28,13 @@
 
 def place(step, lane, side, sign):
     me = lax.axis_index("table")
-    z, y, x = me // (side * side), (me // side) % side, me % side
-    dz, dy, dx = lane, (step // side + lane) % side, (step + lane) % side
+    z, y, x = lax.div(me, side * side), lax.rem(lax.div(me, side), side), lax.rem(me, side)
+    far = lax.div(step, side) if isinstance(step, jax.Array) else step // side
     if sign > 0:
-        z, y, x = (z + dz) % side, (y + dy) % side, (x + dx) % side
+        z, y, x = z + lane, y + far + lane, x + step + lane
     else:
-        z, y, x = (z - dz + side) % side, (y - dy + side) % side, (x - dx + side) % side
-    return (z * side + y) * side + x
+        z, y, x = z - lane + side, y - far - lane + 2 * side, x - step - lane + (side + 1) * side
+    return (lax.rem(z, side) * side + lax.rem(y, side)) * side + lax.rem(x, side)
 
 
 def greet_all(side):
@@ -86,11 +86,11 @@
 def kernel(
     side, cap, block,
     table_in, serve_in, slots_in, lengths, w_proj_in, w_out_in, cotangent_in,
-    layer_out, grad_table,
+    layer_out, own_half, their_half,
     serve, slots, weights_own, w_out, cotangent, picked, send, recv, back, turned, embedded,
     x_all, g_all, gate, value, query, keyrow, slope, grad_gated, attended, stat_send, stat_recv,
     soft, soft_slope, grad_att, grad_q, grad_k, grad_v, gated_own, gated_send, gated_recv,
-    gx_own, gx_send, gx_recv, grads, half_send, half_recv, result,
+    gx_own, gx_send, gx_recv, grads, half_send,
     load_sem, store_sem, out_sem, in_sem, back_out_sem, back_in_sem, core_out_sem, core_in_sem,
 ):
     table, core = lax.axis_index("table"), lax.axis_index("ctx")
@@ -118,10 +118,12 @@
         pltpu.make_async_copy(src, dst, load_sem.at[number])
         for number, (src, dst) in enumerate(loads)
     ]
-    for load in loads:
+    for load in loads[:2]:
         load.start()
     greet_all(side)
     pl.semaphore_signal(barrier, inc=1, device_id=other, device_id_type=MESH)
+    for load in loads[2:]:
+        load.start()
 
     rounded = keyrow
     loads[0].wait()
@@ -145,12 +147,15 @@
         for lane in range(first_lane, side):
             ask(step, lane).start()
 
-    pick(0)
+    early = 2
+    for step in range(early):
+        pick(step)
     pl.semaphore_wait(barrier, side**3)
+    for step in range(early):
+        start_ask(step, 1 if step == 0 else 0)
     recv[0:cap, :] = send[0:cap, :]
-    start_ask(0, 1)
-
-    @pl.loop(1, steps)
+
+    @pl.loop(early, steps)
     def _(step):
         pick(step)
         start_ask(step, 0)
@@ -159,6 +164,8 @@
         load.wait()
 
     def rows_of(index):
+        if isinstance(index, int):
+            return pl.ds(index * block, block)
         return pl.ds(pl.multiple_of(index * block, block), block)
 
     def valid(index, height):
@@ -264,7 +271,7 @@
 
     def pair_ref(ref, i, number, j):
         row = (((i % 2) * heads + number) * blocks + j) * block
-        return ref.at[pl.ds(pl.multiple_of(row, block), block)]
+        return ref.at[pl.ds(row, block)]
 
     def forward_pair(i, j, masked):
         for number in range(heads):
@@ -295,8 +302,7 @@
         here = rows_of(i)
         grad_gated[i % 2] = dot(g_all[here, :], w_out[pl.ds(own_cols, cols), :], NT)
 
-        @pl.loop(0, i)
-        def _(j):
+        for j in range(i):
             forward_pair(i, j, False)
 
         att = attended[i % 2]
@@ -359,8 +365,7 @@
         combine(i)
         grad_q[...] = jnp.zeros_like(grad_q)
 
-        @pl.loop(0, i + 1)
-        def _(j):
+        for j in range(i + 1):
             backward_pair(i, j)
 
         here = rows_of(i)
@@ -384,13 +389,12 @@
 
         @pl.when(jnp.logical_not(is_own(i)))
         def _():
-            gx_send[local, :] = total
+            gx_send[local, :] = total.astype(BF16)
             send_gx(i % own_blocks).start()
 
     forward(blocks - 1)
 
-    @pl.loop(0, blocks - 1)
-    def _(step):
+    for step in range(blocks - 1):
         forward(blocks - 2 - step)
         backward(blocks - 1 - step)
 
@@ -410,7 +414,7 @@
         here = rows_of(index)
         normal_x, inverse = normalize(index)
         send_gx(index).wait_recv()
-        grad_x = gx_own[here, :] + gx_recv[here, :]
+        grad_x = gx_own[here, :] + gx_recv[here, :].astype(F32)
         middle = jnp.mean(grad_x, axis=-1, keepdims=True)
         along = jnp.mean(grad_x * normal_x, axis=-1, keepdims=True)
         masked = g_all[rows_of(first + index), :].astype(F32)
@@ -426,18 +430,19 @@
     def sums_back(step):
         for lane in range(side):
             base = place(step, lane, side, 1) * cap
-            row = pl.multiple_of((step * side + lane) * cap, cap)
-            send[pl.ds(row, cap), :] = dot(
-                multi_hot(slots, base, cap, 0, positions), grads[...]
-            ).astype(BF16)
+            picked[lane * cap : (lane + 1) * cap, 0:positions] = multi_hot(
+                slots, base, cap, 0, positions
+            )
+        row = pl.multiple_of(step * lanes, lanes)
+        send[pl.ds(row, lanes), :] = dot(picked[:, 0:positions], grads[...]).astype(BF16)
 
     def start_give(step, first_lane):
         for lane in range(first_lane, side):
             give(step, lane).start()
 
     sums_back(0)
+    start_give(0, 1)
     back[0:cap, :] = send[0:cap, :]
-    start_give(0, 1)
 
     @pl.loop(1, steps)
     def _(step):
@@ -466,8 +471,10 @@
     mine = pl.ds(pl.multiple_of(core * half, half), half)
     theirs = pl.ds(pl.multiple_of((1 - core) * half, half), half)
     half_send[...] = total[theirs, :].astype(BF16)
-    swap = copy_over(half_send, half_recv, at_half)
+    swap = copy_over(half_send, their_half, at_half)
     swap.start()
+    last = pltpu.make_async_copy(total.at[mine], own_half, store_sem.at[1])
+    last.start()
 
     def given(step, first_lane):
         for lane in range(first_lane, side):
@@ -484,12 +491,58 @@
     def _(i):
         send_stat(i).wait_send()
 
-    swap.wait()
-    result[...] = total[mine, :] + half_recv[...].astype(F32)
-    last = pltpu.make_async_copy(result, grad_table, store_sem.at[1])
-    last.start()
     store.wait()
     last.wait()
+    swap.wait()
+
+
+def finish_kernel(rows, own, their, rows_out, total_out, held, mine, theirs, load_sem, store_sem):
+    half = own.shape[0] // 2
+    loads = []
+    for part in range(2):
+        here = slice(part * half, (part + 1) * half)
+        for number, (src, dst) in enumerate(((own, mine), (their, theirs))):
+            loads.append(
+                pltpu.make_async_copy(src.at[here], dst.at[here], load_sem.at[2 * part + number])
+            )
+    loads.append(pltpu.make_async_copy(rows, held, load_sem.at[4]))
+    for load in loads:
+        load.start()
+    stores = []
+    for part in range(2):
+        here = slice(part * half, (part + 1) * half)
+        loads[2 * part].wait()
+        loads[2 * part + 1].wait()
+        mine[here, :] = mine[here, :] + theirs[here, :].astype(F32)
+        stores.append(pltpu.make_async_copy(mine.at[here], total_out.at[here], store_sem.at[part]))
+        stores[-1].start()
+    loads[4].wait()
+    stores.append(pltpu.make_async_copy(held, rows_out, store_sem.at[2]))
+    stores[-1].start()
+    for store in stores:
+        store.wait()
+
+
+def finish(rows, own, their):
+    anywhere = pl.BlockSpec(memory_space=pl.ANY)
+    return pl.pallas_call(
+        finish_kernel,
+        out_shape=(
+            jax.ShapeDtypeStruct(rows.shape, rows.dtype),
+            jax.ShapeDtypeStruct(own.shape, own.dtype),
+        ),
+        in_specs=[anywhere] * 3,
+        out_specs=(anywhere, anywhere),
+        scratch_shapes=[
+            pltpu.VMEM(rows.shape, rows.dtype),
+            pltpu.VMEM(own.shape, own.dtype),
+            pltpu.VMEM(their.shape, their.dtype),
+            pltpu.SemaphoreType.DMA((5,)),
+            pltpu.SemaphoreType.DMA((3,)),
+        ],
+        compiler_params=pltpu.CompilerParams(vmem_limit_bytes=63 << 20),
+        name="finish",
+    )(rows, own, their)
 
 
 def on_device(side, item_table, serve_rows, token_slots, lengths, w_proj, w_out, grad_out):
@@ -548,12 +601,10 @@
         "gated_send": rows_b(positions, cols),
         "gated_recv": rows_b(positions, cols),
         "gx_own": rows_f(positions, width),
-        "gx_send": rows_f(positions, width),
-        "gx_recv": rows_f(positions, width),
+        "gx_send": rows_b(positions, width),
+        "gx_recv": rows_b(positions, width),
         "grads": rows_b(positions, width),
         "half_send": rows_b(table_rows // 2, width),
-        "half_recv": rows_b(table_rows // 2, width),
-        "result": rows_f(table_rows // 2, width),
         "load_sem": sems((9,)),
         "store_sem": sems((2,)),
         "out_sem": sems((chips,)),
@@ -563,20 +614,22 @@
         "core_out_sem": sems((copies,)),
         "core_in_sem": sems((copies,)),
     }
-    layer_out, grad_table = pl.pallas_call(
+    results = pl.pallas_call(
         functools.partial(kernel, side, cap, block),
         out_shape=(
             jax.ShapeDtypeStruct((positions, width), BF16),
             jax.ShapeDtypeStruct((table_rows // 2, width), F32),
+            jax.ShapeDtypeStruct((table_rows // 2, width), BF16),
         ),
         in_specs=[anywhere] * 3 + [pl.BlockSpec(memory_space=pltpu.SMEM)] + [anywhere] * 3,
-        out_specs=(anywhere, anywhere),
+        out_specs=(anywhere,) * 3,
         scratch_shapes=list(scratch.values()),
         compiler_params=pltpu.CompilerParams(
             collective_id=0, has_side_effects=True, vmem_limit_bytes=63 << 20
         ),
         name="hstu",
     )(item_table, serve_rows, slots, lengths, w_proj, w_out, grad_out[0])
+    layer_out, grad_table = finish(*results)
     return (layer_out[None], grad_table)
 
 

time: 117 us -> 110 us (0.940)
  local copies, waits for them, and re-layouts: 4.13 us -> 0 us
  Pallas kernels: 111 us -> 108 us
    pallas_call x1, Pallas kernels: 111 us -> 106 us  [on_device(): pl.pallas_call(functools.partial(kernel, side, cap, block), out_shape=(ja...]
    unnamed x2 -> x0, local copies, waits for them, and re-layouts: 4.13 us -> none
    pallas_call x0 -> x1, Pallas kernels: none -> 2.42 us  [finish(): pl.pallas_call(finish_kernel, out_shape=(jax.ShapeDtypeStruct(rows.shape,...]
where the time goes in v3:
time: 110 us
  Pallas kernels  108 us (98%)
  between operations  1.47 us (1%)
    pallas_call x1, Pallas kernels, on_device(): pl.pallas_call(functools.partial(kernel, side, cap, block), out_shape=(ja...  106 us
    pallas_call x1, Pallas kernels, finish(): pl.pallas_call(finish_kernel, out_shape=(jax.ShapeDtypeStruct(rows.shape,...  2.42 us

profile of v3, /device:TPU:1, one launch (start us, length us, event | category | flops | bytes accessed | tf_op | source)
XLA Modules:
  0.0 109.5 jit_solution(305332270561744296)
XLA Ops:
  1.3 105.6 %hstu.1 = (bf16[1024,256]{1,0:T(8,128)(2,1)}, f32[1024,256]{1,0:T(8,128)}, bf16[1024,256]{1,0:T(8,128)(2,1)}) custom-call(f32[2048,256]{1,0:T(8,128)} %table_in.1, s32[64,64]{1,0:T(8,128)} %serve_in.1, s32[4,1024]{1,0:T(4,128)} %bitcast.6, s32[1]{0:T(128)S(6)} %copy.9.lengths, bf16[256,2048]{1,0:T(8,128)(2,1)} %w_proj_in.1, bf16[512,256]{1,0:T(8,128)(2,1)} %w_out_in.1, ...), custom_call_target="tpu_custom_call" | custom-call | tf_op jit(solution)/shard_map/hstu/pallas_call | solution.py:617
  106.9 2.4 %finish.1 = (bf16[1024,256]{1,0:T(8,128)(2,1)}, f32[1024,256]{1,0:T(8,128)}) custom-call(bf16[1024,256]{1,0:T(8,128)(2,1)} %get-tuple-element.7.rows, f32[1024,256]{1,0:T(8,128)} %get-tuple-element.8.own, bf16[1024,256]{1,0:T(8,128)(2,1)} %get-tuple-element.9.their), custom_call_target="tpu_custom_call" | custom-call | tf_op jit(solution)/shard_map/finish/pallas_call | solution.py:528
